TPU v7x, 32 devices: a whole 2x2x4 slice. The times are simulated.
32 devices in a mesh: seg: 4 (over y, x), grp: 8 (over z, core).
Axes of the slice: x: 2, y: 2, z: 4, core: 2. Of those that a mesh axis runs over, the one named last changes fastest.
Arguments:
- tile_tokens: bfloat16 [32768, 1536], P(('seg', 'grp')), may hold values from -6 to 6
- gate_weight: bfloat16 [1536, 2048], P(('seg', 'grp')), may hold values from -0.15625 to 0.15625
- up_weight: bfloat16 [1536, 2048], P(('seg', 'grp')), may hold values from -0.15625 to 0.15625
- down_weight: bfloat16 [2048, 1536], P(('seg', 'grp')), may hold values from -0.125 to 0.125
- proj_weight: bfloat16 [1536, 768], replicated, may hold values from -0.15625 to 0.15625
- query_weight: bfloat16 [768, 768], replicated, may hold values from -40 to 40
- key_weight: bfloat16 [768, 768], replicated, may hold values from -1 to 1
- value_weight: bfloat16 [768, 768], replicated, may hold values from -0.21875 to 0.21875
- tile_rank: int32 [32768], P(('seg', 'grp')), may hold values from 0 to 32767, as said below
- valid_count: int32 [1], replicated, may hold values from 16384 to 32767
Outputs:
- attended: bfloat16 [8, 4096, 768], P('grp', 'seg')
Inputs may be any that keep to these rules, and one draw needn't show every extreme that they name: `tile_rank`: A permutation of the positions. Device with seg index s and grp index g holds tiles 1024 * (s * (number of grp devices) + g) onward and positions 4096 * g + 1024 * s onward. At most 64 tiles of one device's batch take positions in one device's block, exactly 64 for some pairs in every draw; that number depends only on the difference of the two devices' flat indices modulo the number of devices.
All inputs are finite; a program needn't handle non-finite values.
Results may differ from a plain program's by a relative error of at most 0.028.
Values may be sent and summed in bfloat16 or wider, within the bound.
A program may use at most 192 MiB of HBM per device.

v0:
```python
import math

import jax
import jax.numpy as jnp
from jax import lax
from jax.sharding import PartitionSpec as P

D = 768
HEADS = 16
LOC = 512
RATE = 4


def passed_along(shard, axis, by):
    devices = lax.axis_size(axis)
    return lax.ppermute(shard, axis, [(i, (i + by) % devices) for i in range(devices)])


def layer_norm(values, epsilon):
    row_mean = jnp.mean(values, axis=-1, keepdims=True)
    centered = values - row_mean
    row_var = jnp.mean(centered * centered, axis=-1, keepdims=True)
    return centered * lax.rsqrt(row_var + epsilon)


def diagonal_rows(values):
    length = values.shape[0]
    shaped = values.reshape(length // RATE, RATE, HEADS // RATE, RATE, D // HEADS)
    picked = jnp.diagonal(shaped, axis1=1, axis2=3)
    return jnp.transpose(picked, (0, 1, 3, 2)).reshape(length // RATE, D)


def fold_rows(left, piece):
    return jnp.dot(left, piece, preferred_element_type=jnp.float32)


def shards(
    tile_tokens,
    gate_weight,
    up_weight,
    down_weight,
    proj_weight,
    query_weight,
    key_weight,
    value_weight,
    tile_rank,
    valid_count,
):
    seg_count = lax.axis_size("seg")
    grp_count = lax.axis_size("grp")
    devices = seg_count * grp_count
    row_count = tile_tokens.shape[0]
    residual = tile_tokens.astype(jnp.float32)
    normed = layer_norm(residual, 1e-06).astype(jnp.bfloat16)
    gate_acc = fold_rows(normed, lax.all_gather(gate_weight, ("seg", "grp"), axis=0, tiled=True))
    up_acc = fold_rows(normed, lax.all_gather(up_weight, ("seg", "grp"), axis=0, tiled=True))
    hidden = (jax.nn.silu(gate_acc) * up_acc).astype(jnp.bfloat16)
    mixed = fold_rows(hidden, lax.all_gather(down_weight, ("seg", "grp"), axis=0, tiled=True))
    final_normed = layer_norm(residual + mixed, 1e-06).astype(jnp.bfloat16)
    embedded = jnp.dot(final_normed, proj_weight, preferred_element_type=jnp.float32).astype(
        jnp.bfloat16
    )
    slot_cap = 2 * row_count // devices
    seg_tok = seg_count * row_count
    target_grp = tile_rank // seg_tok
    target_seg = tile_rank % seg_tok // row_count
    target = target_seg * grp_count + target_grp
    within = tile_rank % row_count
    onehot = (target[:, None] == jnp.arange(devices, dtype=jnp.int32)[None, :]).astype(jnp.int32)
    before = jnp.cumsum(onehot, axis=0) - onehot
    rank_within = jnp.sum(before * onehot, axis=1)
    slot_index = target * slot_cap + rank_within
    send_rows = jnp.zeros((devices * slot_cap, D), jnp.bfloat16).at[slot_index].set(embedded)
    send_place = jnp.full((devices * slot_cap,), -1, jnp.int32).at[slot_index].set(within)
    got_rows, got_place = (
        lax.all_to_all(
            send_rows.reshape(devices, slot_cap, D),
            ("seg", "grp"),
            split_axis=0,
            concat_axis=0,
            tiled=True,
        ),
        lax.all_to_all(
            send_place.reshape(devices, slot_cap),
            ("seg", "grp"),
            split_axis=0,
            concat_axis=0,
            tiled=True,
        ),
    )
    got_rows = got_rows.reshape(devices * slot_cap, D)
    got_place = got_place.reshape(devices * slot_cap)
    landing = jnp.where(got_place >= 0, got_place, row_count)
    source = (
        jnp.zeros((row_count,), jnp.int32)
        .at[landing]
        .set(jnp.arange(devices * slot_cap, dtype=jnp.int32), mode="drop")
    )
    sequence = got_rows[source]
    normed_seq = layer_norm(sequence.astype(jnp.float32), 1e-05).astype(jnp.bfloat16)
    query_rows = jnp.dot(normed_seq, query_weight, preferred_element_type=jnp.float32).astype(
        jnp.bfloat16
    )
    key_rows = jnp.dot(normed_seq, key_weight, preferred_element_type=jnp.float32).astype(
        jnp.bfloat16
    )
    value_rows = jnp.dot(normed_seq, value_weight, preferred_element_type=jnp.float32).astype(
        jnp.bfloat16
    )
    seg_here = lax.axis_index("seg")
    grp_here = lax.axis_index("grp")
    valid_limit = valid_count[0]
    local_pos = grp_here * seg_tok + seg_here * row_count + jnp.arange(row_count, dtype=jnp.int32)
    live_mask = local_pos < valid_limit
    head_size = D // HEADS
    score_scale = 1.0 / math.sqrt(head_size)

    def local_branch(operands):
        query_blk, key_blk, value_blk, keep_blk = operands
        scores = (
            jnp.einsum("qhd,khd->hqk", query_blk, key_blk, preferred_element_type=jnp.float32)
            * score_scale
        )
        allowed = keep_blk[None, None, :] | jnp.eye(LOC, dtype=jnp.bool_)[None]
        scores = jnp.where(allowed, scores, -jnp.inf)
        row_max = jnp.max(scores, axis=-1)
        weights = jnp.exp(scores - row_max[..., None])
        row_total = jnp.sum(weights, axis=-1)
        accum = jnp.einsum(
            "hqk,khd->qhd",
            weights.astype(jnp.bfloat16),
            value_blk,
            preferred_element_type=jnp.float32,
        )
        return (row_max.T, row_total.T, accum)

    block_count = row_count // LOC
    near_max, near_total, near_acc = lax.map(
        local_branch,
        (
            query_rows.reshape(block_count, LOC, HEADS, head_size),
            key_rows.reshape(block_count, LOC, HEADS, head_size),
            value_rows.reshape(block_count, LOC, HEADS, head_size),
            live_mask.reshape(block_count, LOC),
        ),
    )
    sparse_count = row_count // RATE
    query_sparse = diagonal_rows(query_rows).reshape(sparse_count, HEADS, head_size)
    key_sparse = diagonal_rows(key_rows)
    value_sparse = diagonal_rows(value_rows)
    head_phase = jnp.arange(HEADS, dtype=jnp.int32) % RATE
    query_index = seg_here * sparse_count + jnp.arange(sparse_count, dtype=jnp.int32)
    initial = (
        jnp.full((HEADS, sparse_count), -1e30, jnp.float32),
        jnp.zeros((HEADS, sparse_count), jnp.float32),
        jnp.zeros((sparse_count, HEADS, head_size), jnp.float32),
    )
    far_state = initial
    kv_block = jnp.stack([key_sparse, value_sparse])
    for step_index in range(seg_count):
        anchor = (seg_here - step_index) % seg_count
        key_block = kv_block[0]
        value_block = kv_block[1]
        piece_rows = key_block.shape[0]
        key_index = anchor * sparse_count + jnp.arange(piece_rows, dtype=jnp.int32)
        key_pos = grp_here * seg_tok + key_index[:, None] * RATE + head_phase[None, :]
        keep_key = key_pos < valid_limit
        absorb_scores = (
            jnp.einsum(
                "qhd,khd->hqk",
                query_sparse,
                key_block.reshape(piece_rows, HEADS, head_size),
                preferred_element_type=jnp.float32,
            )
            * score_scale
        )
        absorb_allowed = keep_key.T[:, None, :] | (query_index[:, None] == key_index[None, :])[None]
        absorb_scores = jnp.where(absorb_allowed, absorb_scores, -1e30)
        absorb_row_max, absorb_row_total, absorb_accum = far_state
        new_max = jnp.maximum(absorb_row_max, jnp.max(absorb_scores, axis=-1))
        shrink = jnp.exp(absorb_row_max - new_max)
        absorb_weights = jnp.exp(absorb_scores - new_max[..., None])
        absorb_row_total = shrink * absorb_row_total + jnp.sum(absorb_weights, axis=-1)
        added = jnp.einsum(
            "hqk,khd->qhd",
            absorb_weights,
            value_block.reshape(piece_rows, HEADS, head_size).astype(jnp.float32),
            precision=lax.Precision.HIGHEST,
        )
        absorb_accum = shrink.T[..., None] * absorb_accum + added
        far_state = (new_max, absorb_row_total, absorb_accum)
        if step_index + 1 < seg_count:
            kv_block = passed_along(kv_block, "seg", 1)
    far_max, far_total, far_acc = far_state
    group_count = HEADS // RATE
    near_shape = (sparse_count, RATE, group_count, RATE)
    far_shape = (sparse_count, 1, group_count, RATE)
    near_max = near_max.reshape(near_shape)
    near_total = near_total.reshape(near_shape)
    near_acc = near_acc.reshape(near_shape + (head_size,))
    far_max = far_max.T.reshape(far_shape)
    far_total = far_total.T.reshape(far_shape)
    far_acc = far_acc.reshape(far_shape + (head_size,))
    same_phase = jnp.eye(RATE, dtype=jnp.bool_)[:, None, :]
    best_max = jnp.where(same_phase, jnp.maximum(near_max, far_max), near_max)
    near_coef = jnp.exp(near_max - best_max)
    far_coef = jnp.where(same_phase, jnp.exp(jnp.where(same_phase, far_max - best_max, 0.0)), 0.0)
    numerator = near_coef[..., None] * near_acc + far_coef[..., None] * far_acc
    denominator = near_coef * near_total + far_coef * far_total
    attended = (numerator / denominator[..., None]).reshape(row_count, D)
    attended = jnp.where(live_mask[:, None], attended, 0.0).astype(jnp.bfloat16)
    return attended[None]


def solution(mesh):
    return jax.shard_map(
        shards,
        mesh=mesh,
        in_specs=(
            P(("seg", "grp"), None),
            P(("seg", "grp"), None),
            P(("seg", "grp"), None),
            P(("seg", "grp"), None),
            P(),
            P(),
            P(),
            P(),
            P(("seg", "grp")),
            P(),
        ),
        out_specs=P("grp", "seg", None),
        check_vma=False,
    )
```

profile of v0, /device:TPU:0, one launch (start us, length us, event | category | flops | bytes accessed | tf_op | source)
XLA Modules:
  0.0 724.0 jit_solution(6479057405256750491)
XLA Ops:
  9.5 9.0 %reduce-window.6 = s32[32,8,128]{2,1,0:T(8,128)S(1)} reduce-window(s32[32,8,128]{2,1,0:T(8,128)S(1)} %fusion.87, s32[]{:T(128)} %constant.154.clone.1), window={size=1x1x128 pad=0_0x0_0x127_0}, to_apply=%region_0.0 | reduce-window | flops 4161536 | bytes 262148 | tf_op jit(solution)/shard_map/reduce-window
  35.1 47.4 %all-gather.4.cloned.1.call-done = bf16[1536,2048]{1,0:T(8,128)(2,1)} async-done(((bf16[48,2048]{1,0:T(8,128)(2,1)}), bf16[1536,2048]{1,0:T(8,128)(2,1)}) %all-gather.4.cloned.1.call-update) | async-done | bytes 6291472 | tf_op jit(solution)/shard_map/all_gather | solution.py:55
  82.5 12.4 %fusion.115 = f32[1024,2048]{1,0:T(8,128)} fusion(bf16[1536,2048]{1,0:T(8,128)(2,1)} %all-gather.4.cloned.1.call-done, bf16[1024,1536]{1,0:T(8,128)(2,1)} %param.12, f32[1024]{0:T(1024)S(1)} %add_rsqrt_fusion.2, f32[1024]{0:T(1024)S(1)} %broadcast_multiply_fusion.3), kind=kOutput, calls=%fused_computation.207 | convolution fusion | flops 6448742400 | bytes 17833984 | tf_op jit(solution)/shard_map/dot_general | solution.py:34
  94.9 58.6 %all-gather.6.cloned.1.call-done = bf16[1536,2048]{1,0:T(8,128)(2,1)} async-done(((bf16[48,2048]{1,0:T(8,128)(2,1)}), bf16[1536,2048]{1,0:T(8,128)(2,1)}) %all-gather.6.cloned.1.call-update) | async-done | bytes 6291472 | tf_op jit(solution)/shard_map/all_gather | solution.py:56
  153.5 71.0 %all-gather.8.cloned.1.call-done = bf16[2048,1536]{1,0:T(8,128)(2,1)} async-done(((bf16[64,1536]{1,0:T(8,128)(2,1)}), bf16[2048,1536]{1,0:T(8,128)(2,1)}) %all-gather.8.cloned.1.call-update) | async-done | bytes 6291472 | tf_op jit(solution)/shard_map/all_gather | solution.py:58
  224.5 23.5 %fusion.127 = (f32[1024]{0:T(1024)S(1)}, f32[1024,1536]{1,0:T(8,128)}) fusion(bf16[2048,1536]{1,0:T(8,128)(2,1)} %all-gather.8.cloned.1.call-done, bf16[1024,1536]{1,0:T(8,128)(2,1)} %param.12, f32[1024,2048]{1,0:T(8,128)} %fusion.115, bf16[1536,2048]{1,0:T(8,128)(2,1)} %all-gather.6.cloned.1.call-done, f32[1024]{0:T(1024)S(1)} %add_rsqrt_fusion.2, ...), kind=kOutput, calls=%fused_computation.212 | convolution fusion | flops 12908493824 | bytes 30420992 | tf_op jit(solution)/shard_map/dot_general | solution.py:34
  256.6 17.9 %scatter_custom_fusion = bf16[2048,768]{1,0:T(8,128)(2,1)} fusion(s32[1024]{0:T(1024)S(1)} %compare_select_fusion.3, bf16[1024,768]{1,0:T(8,128)(2,1)} %fusion.70, bf16[]{:T(256)} %constant.156.clone.1), kind=kCustom, calls=%fused_computation.102 | custom fusion | bytes 3146240 | tf_op jit(solution)/shard_map/scatter | solution.py:73
  289.4 61.2 %all-to-all-done = bf16[32,64,768]{2,1,0:T(8,128)(2,1)} async-done(((bf16[32,64,768]{2,1,0:T(8,128)(2,1)}), bf16[32,64,768]{2,1,0:T(8,128)(2,1)}, u32[]{:S(2)}, u32[]{:S(2)}) %all-to-all-start) | async-done | bytes 3145760 | tf_op jit(solution)/shard_map/all_to_all | solution.py:76
  365.0 10.5 %reshape.590 = bf16[256,4,4,4,48]{4,3,2,1,0:T(4,128)(2,1)} reshape(bf16[1024,768]{1,0:T(8,128)(2,1)} %convolution_convert_fusion.1) | data formatting | bytes 3145728 | tf_op jit(solution)/shard_map/reshape | solution.py:28
  382.0 10.5 %reshape.591 = bf16[256,4,4,4,48]{4,3,2,1,0:T(4,128)(2,1)} reshape(bf16[1024,768]{1,0:T(8,128)(2,1)} %convolution_convert_fusion) | data formatting | bytes 3145728 | tf_op jit(solution)/shard_map/reshape | solution.py:28
  431.2 115.6 %while.14 = (s32[]{:T(128)}, f32[2,512,16]{1,0,2:T(2,128)S(1)}, f32[2,512,16]{1,0,2:T(2,128)S(1)}, f32[2,512,16,48]{1,0,3,2:T(2,128)}, pred[2,512]{1,0:T(4,128)(...) while((s32[]{:T(128)}, f32[2,512,16]{1,0,2:T(2,128)S(1)}, ...), condition=%wide.region_15.16_spmd, body=%wide.region_12.15_spmd.sunk | while | flops 851951616 | bytes 61999744 | solution.py:138
  431.4 9.7 %fusion.165 = (f32[16,512]{1,0:T(8,128)S(1)}, f32[16,512,512]{1,2,0:T(8,128)}) fusion(pred[512,512]{0,1:T(8,128)(4,1)S(1)} %fusion.164, bf16[2,512,16,48]{1,3,2,0:T(8,128)(2,1)} %get-tuple-element.220, s32[]{:T(128)S(6)} %copy.119, bf16[2,512,16,48]{1,3,2,0:T(8,128)(2,1)} %get-tuple-element.219), kind=kOutput, calls=%fused_computation.9.clone.1 | convolution fusion | flops 415227904 | bytes 18646016 | tf_op jit(solution)/shard_map/while/body/eval_jaxpr/qhd,khd->hqk/dot_general | solution.py:121
  441.3 9.1 %fusion.166 = f32[16,512]{1,0:T(8,128)S(1)} fusion(f32[16,512,512]{1,2,0:T(8,128)} %get-tuple-element.193, f32[16,512]{1,0:T(8,128)S(1)} %get-tuple-element.192, pred[512,512]{0,1:T(8,128)(4,1)S(1)} %fusion.164), kind=kLoop, calls=%fused_computation.11.clone.1 | loop fusion | flops 16769024 | bytes 17104896 | tf_op jit(solution)/shard_map/while/body/eval_jaxpr/reduce_sum | solution.py:128
  460.3 28.7 %dynamic_update_slice.16 = f32[2,512,16,48]{1,0,3,2:T(2,128)} dynamic-update-slice(f32[2,512,16,48]{1,0,3,2:T(2,128)} %get-tuple-element.207, f32[1,512,16,48]{1,0,3,2:T(1,128)S(1)} %copy.111, s32[]{:T(128)S(6)} %copy.119, s32[]{:T(128)} %constant.154.clone.1..sunk, s32[]{:T(128)} %constant.154.clone.1..sunk, s32[]{:T(128)} %constant.154.clone.1..sunk) | dynamic-update-slice | bytes 3145732 | tf_op jit(solution)/shard_map/while/body/jit(dynamic_update_index_in_dim)/dynamic_update_slice | solution.py:138
  489.1 9.7 %fusion.165 = (f32[16,512]{1,0:T(8,128)S(1)}, f32[16,512,512]{1,2,0:T(8,128)}) fusion(pred[512,512]{0,1:T(8,128)(4,1)S(1)} %fusion.164, bf16[2,512,16,48]{1,3,2,0:T(8,128)(2,1)} %get-tuple-element.220, s32[]{:T(128)S(6)} %copy.119, bf16[2,512,16,48]{1,3,2,0:T(8,128)(2,1)} %get-tuple-element.219), kind=kOutput, calls=%fused_computation.9.clone.1 | convolution fusion | flops 415227904 | bytes 18646016 | tf_op jit(solution)/shard_map/while/body/eval_jaxpr/qhd,khd->hqk/dot_general | solution.py:121
  499.1 9.1 %fusion.166 = f32[16,512]{1,0:T(8,128)S(1)} fusion(f32[16,512,512]{1,2,0:T(8,128)} %get-tuple-element.193, f32[16,512]{1,0:T(8,128)S(1)} %get-tuple-element.192, pred[512,512]{0,1:T(8,128)(4,1)S(1)} %fusion.164), kind=kLoop, calls=%fused_computation.11.clone.1 | loop fusion | flops 16769024 | bytes 17104896 | tf_op jit(solution)/shard_map/while/body/eval_jaxpr/reduce_sum | solution.py:128
  518.1 28.7 %dynamic_update_slice.16 = f32[2,512,16,48]{1,0,3,2:T(2,128)} dynamic-update-slice(f32[2,512,16,48]{1,0,3,2:T(2,128)} %get-tuple-element.207, f32[1,512,16,48]{1,0,3,2:T(1,128)S(1)} %copy.111, s32[]{:T(128)S(6)} %copy.119, s32[]{:T(128)} %constant.154.clone.1..sunk, s32[]{:T(128)} %constant.154.clone.1..sunk, s32[]{:T(128)} %constant.154.clone.1..sunk) | dynamic-update-slice | bytes 3145732 | tf_op jit(solution)/shard_map/while/body/jit(dynamic_update_index_in_dim)/dynamic_update_slice | solution.py:138
  546.8 10.7 %reshape.589 = bf16[256,4,4,4,48]{4,3,2,1,0:T(4,128)(2,1)} reshape(bf16[1024,768]{1,0:T(8,128)(2,1)} %convolution_convert_fusion.2) | data formatting | bytes 3145728 | tf_op jit(solution)/shard_map/reshape | solution.py:28
  589.0 13.8 %collective-permute-done.2 = bf16[2,256,768]{1,2,0:T(8,128)(2,1)S(1)} collective-permute-done((bf16[2,256,768]{1,2,0:T(8,128)(2,1)}, bf16[2,256,768]{1,2,0:T(8,128)(2,1)S(1)}, u32[]{:S(2)}, u32[]{:S(2)}) %collective-permute-start.2) | collective-permute-done | bytes 786464 | tf_op jit(solution)/shard_map/ppermute | solution.py:16
  639.6 8.9 %copy.71 = f32[256,4,4,4]{3,2,1,0:T(4,128)} copy(f32[256,4,4,4]{1,0,3,2:T(8,128)} %get-tuple-element.93) | data formatting | bytes 131072 | tf_op jit(solution)/shard_map/exp | solution.py:206
  664.4 10.2 %mul.285 = f32[1,1024,768]{2,1,0:T(8,128)} reshape(f32[256,4,4,4,48]{4,3,2,1,0:T(4,128)} %broadcast_multiply_fusion) | data formatting | bytes 6291456 | tf_op jit(solution)/shard_map/mul | solution.py:208
  674.6 8.8 %mul.270 = f32[256,4,4,4,48]{4,3,2,1,0:T(4,128)} broadcast(f32[256,4,4,4]{3,2,1,0:T(4,128)} %copy.71), dimensions={0,1,2,3} | broadcast | bytes 3211264 | tf_op jit(solution)/shard_map/mul | solution.py:208
  683.4 10.2 %mul.271 = f32[1,1024,768]{2,1,0:T(8,128)} reshape(f32[256,4,4,4,48]{4,3,2,1,0:T(4,128)} %mul.270) | data formatting | bytes 6291456 | tf_op jit(solution)/shard_map/mul | solution.py:208
  700.6 10.3 %div.78 = f32[1,1024,768]{2,1,0:T(8,128)} reshape(f32[256,4,4,4,48]{4,3,2,1,0:T(4,128)} %div.77) | data formatting | bytes 6291456 | tf_op jit(solution)/shard_map/div | solution.py:210
  (191 shorter events, 219.5 us)
Async XLA Ops:
  6.5 245.1 %copy-start = (bf16[1536,768]{1,0:T(8,128)(2,1)S(1)}, bf16[1536,768]{1,0:T(8,128)(2,1)}, u32[]{:S(2)}) copy-start(bf16[1536,768]{1,0:T(8,128)(2,1)} %param.16) | copy-start | bytes 7077892
  6.5 76.0 %all-gather.4.cloned.1.call-start = ((), (), s32[]{:S(2)}) async-start(), calls=%async_computation.2 | async-start | bytes 6488064 | tf_op jit(solution)/shard_map/all_gather | solution.py:55
  7.3 146.2 %all-gather.6.cloned.1.call-start = ((), (), s32[]{:S(2)}) async-start(), calls=%async_computation.3 | async-start | bytes 6488064 | tf_op jit(solution)/shard_map/all_gather | solution.py:56
  8.0 216.5 %all-gather.8.cloned.1.call-start = ((), (), s32[]{:S(2)}) async-start(), calls=%async_computation.4 | async-start | bytes 6488064 | tf_op jit(solution)/shard_map/all_gather | solution.py:58
  24.0 250.5 %all-to-all-start.1 = ((s32[32,1,64]{2,1,0:T(1,128)}), s32[32,1,64]{2,1,0:T(1,128)S(1)}, u32[]{:S(2)}, u32[]{:S(2)}) async-start(s32[32,1,64]{2,1,0:T(1,128)} %all_to_all.10), calls=%async_computation.1 | async-start | bytes 32768 | tf_op jit(solution)/shard_map/all_to_all | solution.py:83
  274.5 76.2 %all-to-all-start = ((bf16[32,64,768]{2,1,0:T(8,128)(2,1)}), bf16[32,64,768]{2,1,0:T(8,128)(2,1)}, u32[]{:S(2)}, u32[]{:S(2)}) async-start(bf16[32,64,768]{2,1,0:T(8,128)(2,1)} %bitcast.233), calls=%async_computation | async-start | bytes 6291456 | tf_op jit(solution)/shard_map/all_to_all | solution.py:76
  399.0 7.3 %copy-start.3 = (bf16[1024,768]{1,0:T(8,128)(2,1)S(1)}, bf16[1024,768]{1,0:T(8,128)(2,1)}, u32[]{:S(2)}) copy-start(bf16[1024,768]{1,0:T(8,128)(2,1)} %copy-done.2) | copy-start | bytes 4718596
  399.1 30.1 %collective-permute-start = (bf16[2,256,768]{1,2,0:T(8,128)(2,1)S(1)}, bf16[2,256,768]{1,2,0:T(8,128)(2,1)}, u32[]{:S(2)}, u32[]{:S(2)}) collective-permute-start(bf16[2,256,768]{1,2,0:T(8,128)(2,1)S(1)} %pad_maximum_fusion), channel_id=1, source_target_pairs={{0,8},{8,16},{16,24},{24,0},{1,9},{9,17},{17,25},{25,1},{2,10},{10... | collective-permute-start | bytes 2359304 | tf_op jit(solution)/shard_map/ppermute | solution.py:16
  414.2 9.8 %copy-start.6 = (bf16[1024,768]{0,1:T(8,128)(2,1)S(1)}, bf16[1024,768]{0,1:T(8,128)(2,1)}, u32[]{:S(2)}) copy-start(bf16[1024,768]{0,1:T(8,128)(2,1)} %copy.58) | copy-start | bytes 4718596
  429.2 153.2 %collective-permute-start.1 = (bf16[2,256,768]{1,2,0:T(8,128)(2,1)}, bf16[2,256,768]{1,2,0:T(8,128)(2,1)}, u32[]{:S(2)}, u32[]{:S(2)}) collective-permute-start(bf16[2,256,768]{1,2,0:T(8,128)(2,1)} %collective-permute-done), channel_id=1, source_target_pairs={{0,8},{8,16},{16,24},{24,0},{1,9},{9,17},{17,25},{25,1},{2,10},{10... | collective-permute-start | bytes 2359304 | tf_op jit(solution)/shard_map/ppermute | solution.py:16
  546.7 16.6 %copy-start.20 = (f32[2,512,16]{1,0,2:T(2,128)}, f32[2,512,16]{1,0,2:T(2,128)S(1)}, u32[]{:S(2)}) copy-start(f32[2,512,16]{1,0,2:T(2,128)S(1)} %get-tuple-element.51) | copy-start | bytes 196612
  546.8 16.6 %copy-start.22 = (f32[2,512,16]{1,0,2:T(2,128)}, f32[2,512,16]{1,0,2:T(2,128)S(1)}, u32[]{:S(2)}) copy-start(f32[2,512,16]{1,0,2:T(2,128)S(1)} %get-tuple-element.49) | copy-start | bytes 196612
  569.6 9.5 %copy-start.19 = (pred[256,256]{0,1:T(8,128)(4,1)S(1)}, pred[256,256]{0,1:T(8,128)(4,1)}, u32[]{:S(2)}) copy-start(pred[256,256]{0,1:T(8,128)(4,1)} %get-tuple-element.115) | copy-start | bytes 196612
  569.6 9.5 %copy-start.27 = (pred[16,256]{1,0:T(8,128)(4,1)S(1)}, pred[16,256]{1,0:T(8,128)(4,1)}, u32[]{:S(2)}) copy-start(pred[16,256]{1,0:T(8,128)(4,1)} %get-tuple-element.119) | copy-start | bytes 12292
  575.4 7.9 %copy-start.18 = (pred[256,256]{0,1:T(8,128)(4,1)S(1)}, pred[256,256]{0,1:T(8,128)(4,1)}, u32[]{:S(2)}) copy-start(pred[256,256]{0,1:T(8,128)(4,1)} %get-tuple-element.116) | copy-start | bytes 196612
  575.4 7.9 %copy-start.26 = (pred[16,256]{1,0:T(8,128)(4,1)S(1)}, pred[16,256]{1,0:T(8,128)(4,1)}, u32[]{:S(2)}) copy-start(pred[16,256]{1,0:T(8,128)(4,1)} %get-tuple-element.120) | copy-start | bytes 12292
  580.5 29.3 %copy-start.7 = (f32[16,256,256]{1,2,0:T(8,128)}, f32[16,256,256]{1,2,0:T(8,128)S(1)}, u32[]{:S(2)}) copy-start(f32[16,256,256]{1,2,0:T(8,128)S(1)} %get-tuple-element.132) | copy-start | bytes 12582916
  582.4 20.4 %collective-permute-start.2 = (bf16[2,256,768]{1,2,0:T(8,128)(2,1)}, bf16[2,256,768]{1,2,0:T(8,128)(2,1)S(1)}, u32[]{:S(2)}, u32[]{:S(2)}) collective-permute-start(bf16[2,256,768]{1,2,0:T(8,128)(2,1)} %collective-permute-done.1), channel_id=1, source_target_pairs={{0,8},{8,16},{16,24},{24,0},{1,9},{9,17},{17,25},{25,1},{2,10},{10... | collective-permute-start | bytes 2359304 | tf_op jit(solution)/shard_map/ppermute | solution.py:16
  584.8 23.5 %copy-start.10 = (f32[16,256,256]{1,2,0:T(8,128)}, f32[16,256,256]{1,2,0:T(8,128)S(1)}, u32[]{:S(2)}) copy-start(f32[16,256,256]{1,2,0:T(8,128)S(1)} %get-tuple-element.130) | copy-start | bytes 12582916
  584.8 18.8 %copy-start.16 = (pred[256,256]{0,1:T(8,128)(4,1)S(1)}, pred[256,256]{0,1:T(8,128)(4,1)}, u32[]{:S(2)}) copy-start(pred[256,256]{0,1:T(8,128)(4,1)} %get-tuple-element.118) | copy-start | bytes 196612
  584.8 18.8 %copy-start.24 = (pred[16,256]{1,0:T(8,128)(4,1)S(1)}, pred[16,256]{1,0:T(8,128)(4,1)}, u32[]{:S(2)}) copy-start(pred[16,256]{1,0:T(8,128)(4,1)} %get-tuple-element.122) | copy-start | bytes 12292
  589.0 17.7 %copy-start.8 = (f32[16,256,256]{1,2,0:T(8,128)}, f32[16,256,256]{1,2,0:T(8,128)S(1)}, u32[]{:S(2)}) copy-start(f32[16,256,256]{1,2,0:T(8,128)S(1)} %get-tuple-element.128) | copy-start | bytes 12582916
  700.6 10.3 %copy-start.28 = (pred[1024]{0:T(1024)(128)(4,1)S(1)}, pred[1024]{0:T(1024)(128)(4,1)}, u32[]{:S(2)}) copy-start(pred[1024]{0:T(1024)(128)(4,1)} %add_compare_fusion.5) | copy-start | bytes 3076
  700.6 16.7 %copy-start.1 = (bf16[1536,768]{1,0:T(8,128)(2,1)S(1)}, bf16[1536,768]{1,0:T(8,128)(2,1)}, u32[]{:S(2)}) copy-start(bf16[1536,768]{1,0:T(8,128)(2,1)} %param.16) | copy-start | bytes 7077892
  (15 other events, 63.7 us)
Sparse Core Ops, SparseCore 0:
  10.4 72.1 all-gather.3
  85.5 67.9 all-gather.5
  156.5 67.9 all-gather.7
where the time goes:
time: 734 us; the launch traced here: 724 us
  local copies, waits for them, and re-layouts  271 us (37%)
  waiting for transfers between devices  254 us (35%)
  matrix products  105 us (14%)
  other arithmetic  65.3 us (9%)
  between operations  14.7 us (2%)
  starting transfers between devices  13.8 us (2%)
    all_gather x1, waiting for transfers between devices, shards(): lax.all_gather(down_weight, ('seg', 'grp'), axis=0, tiled=True)  71 us
    dynamic_update_slice x12, local copies, waits for them, and re-layouts, shards(): lax.map(local_branch, (query_rows.reshape(block_count, LOC, HEADS, head_s...  61.4 us
    all_to_all x1, waiting for transfers between devices, shards(): lax.all_to_all(send_rows.reshape(devices, slot_cap, D), ('seg', 'grp'), s...  61.2 us
    all_gather x1, waiting for transfers between devices, shards(): lax.all_gather(up_weight, ('seg', 'grp'), axis=0, tiled=True)  58.6 us
    reshape x6, local copies, waits for them, and re-layouts, diagonal_rows(): values.reshape(length // RATE, RATE, HEADS // RATE, RATE, D // HEADS)  49.3 us
    all_gather x1, waiting for transfers between devices, shards(): lax.all_gather(gate_weight, ('seg', 'grp'), axis=0, tiled=True)  47.4 us
    dot_general x2, matrix products, fold_rows(): return jnp.dot(left, piece, preferred_element_type=jnp.float32)  35.8 us
    mul x4, local copies, waits for them, and re-layouts, shards(): numerator = near_coef[..., None] * near_acc + far_coef[..., None] * far_acc  30.9 us
  transfers between devices with their start and end apart: 8, of which 5 were waited for; matrix products, arithmetic and copies ran while one was open for 38% of the time, Pallas kernels for 0%

commit v1 on v0

v1 whole, which is shorter than its diff:
```python
import math

import jax
import jax.numpy as jnp
import numpy as np
from jax import lax
from jax.experimental import pallas as pl
from jax.experimental.pallas import tpu as pltpu
from jax.sharding import PartitionSpec as P

D = 768
HEADS = 16
LOC = 512
RATE = 4
HEAD = D // HEADS
PER_PHASE = HEADS // RATE
LANES = 256
PACKED = 384
PHASE_ROWS = LOC // RATE
EXP_SCALE = math.log2(math.e) / math.sqrt(HEAD)
MASKED = -1e30
VMEM_LIMIT = 56 * 1024 * 1024


def layer_norm(values, epsilon):
    row_mean = jnp.mean(values, axis=-1, keepdims=True)
    centered = values - row_mean
    row_var = jnp.mean(centered * centered, axis=-1, keepdims=True)
    return centered * lax.rsqrt(row_var + epsilon)


def fold_rows(left, piece):
    return jnp.dot(left, piece, preferred_element_type=jnp.float32)


def lane_sources():
    key_src = np.full((RATE, LANES), -1, np.int32)
    value_src = np.full((RATE, LANES), -1, np.int32)
    for phase in range(RATE):
        for dim in range(PER_PHASE * HEAD):
            source = (dim // HEAD * RATE + phase) * HEAD + dim % HEAD
            key_src[phase, dim] = source
            value_src[phase, dim if dim < 128 else dim + 64] = source
    return key_src.reshape(1, -1), value_src.reshape(1, -1)


def key_lanes(head):
    lane = lax.broadcasted_iota(jnp.int32, (1, LANES), 1)
    return (lane >= head * HEAD) & (lane < (head + 1) * HEAD)


def value_lanes(head):
    lane = lax.broadcasted_iota(jnp.int32, (1, LANES), 1)
    dim = jnp.where(lane < 128, lane, jnp.where(lane >= 192, lane - 64, -1))
    return (dim >= head * HEAD) & (dim < (head + 1) * HEAD)


def qkv_kernel(
    rows_ref, place_ref, key_src_ref, value_src_ref, wq_ref, wk_ref, wv_ref,
    q_ref, k_ref, v_ref, kv_ref,
):
    row_count = q_ref.shape[0]
    column = lax.broadcasted_iota(jnp.int32, (D, RATE * LANES), 0)
    pick_key = (column == key_src_ref[...]).astype(jnp.bfloat16)
    pick_value = (column == value_src_ref[...]).astype(jnp.bfloat16)
    wq = fold_rows(wq_ref[...], pick_key).astype(jnp.bfloat16)
    wk = fold_rows(wk_ref[...], pick_key).astype(jnp.bfloat16)
    wv = fold_rows(wv_ref[...], pick_value).astype(jnp.bfloat16)
    place = place_ref[...]
    spare = value_src_ref[...] < 0
    for start in range(0, row_count, LOC):
        here = lax.broadcasted_iota(jnp.int32, (LOC, place.shape[1]), 0) + start
        pick = (here == place).astype(jnp.bfloat16)
        seq = fold_rows(pick, rows_ref[...])
        normed = layer_norm(seq, 1e-05).astype(jnp.bfloat16)
        block = pl.ds(start, LOC)
        q_ref[block, :] = fold_rows(normed, wq).astype(jnp.bfloat16)
        key = fold_rows(normed, wk).astype(jnp.bfloat16)
        value = jnp.where(spare, 1.0, fold_rows(normed, wv)).astype(jnp.bfloat16)
        k_ref[block, :] = key
        v_ref[block, :] = value
        low = lax.broadcasted_iota(jnp.int32, (PHASE_ROWS, 128), 1) < 64
        for phase in range(RATE):
            kp = key[phase * PHASE_ROWS:(phase + 1) * PHASE_ROWS, phase * LANES:(phase + 1) * LANES]
            vp = value[phase * PHASE_ROWS:(phase + 1) * PHASE_ROWS, phase * LANES:(phase + 1) * LANES]
            out = pl.ds(start // RATE, PHASE_ROWS)
            at = phase * PACKED
            kv_ref[out, at:at + 128] = kp[:, :128]
            kv_ref[out, at + 128:at + 256] = jnp.where(low, kp[:, 128:], vp[:, 128:])
            kv_ref[out, at + 256:at + 384] = vp[:, :128]


def near_kernel(where_ref, q_ref, k_ref, v_ref, near_ref):
    live = where_ref[0] - pl.program_id(0) * LOC
    key_row = lax.broadcasted_iota(jnp.int32, (LOC, LOC), 1)
    query_row = lax.broadcasted_iota(jnp.int32, (LOC, LOC), 0)
    key_pos = (key_row & (PHASE_ROWS - 1)) * RATE + key_row // PHASE_ROWS
    allowed = (key_pos < live) | (key_row == query_row)
    bias = jnp.where(allowed, 0.0, MASKED)
    query, key, value = q_ref[...], k_ref[...], v_ref[...]
    lane = lax.broadcasted_iota(jnp.int32, (1, LANES), 1)
    result = jnp.zeros((LOC, LANES), jnp.float32)
    for head in range(PER_PHASE):
        own = jnp.where(key_lanes(head), query, jnp.zeros_like(query))
        scores = lax.dot_general(
            own, key, (((1,), (1,)), ((), ())), preferred_element_type=jnp.float32
        ) + bias
        top = jnp.max(scores, axis=1, keepdims=True)
        weights = jnp.exp2((scores - top) * EXP_SCALE)
        acc = fold_rows(weights.astype(jnp.bfloat16), value)
        result = jnp.where(value_lanes(head) | (lane == 128 + head), acc, result)
        result = jnp.where(lane == 132 + head, top, result)
    near_ref[...] = result


def far_kernel(where_ref, value_src_ref, q_ref, near_ref, kv_ref, out_ref, att_ref, sum_ref):
    phase = pl.program_id(0)
    row_count = q_ref.shape[0]
    sparse = row_count // RATE
    key_count = kv_ref.shape[0] * kv_ref.shape[1]
    lane = lax.broadcasted_iota(jnp.int32, (1, LANES), 1)
    starts = [pl.multiple_of(base + phase * PHASE_ROWS, PHASE_ROWS) for base in range(0, row_count, LOC)]
    query = jnp.concatenate([q_ref[pl.ds(at, PHASE_ROWS), :] for at in starts], axis=0)
    near_own = jnp.concatenate([near_ref[pl.ds(at, PHASE_ROWS), :] for at in starts], axis=0)
    packed = kv_ref[...].reshape(key_count, PACKED)
    key = packed[:, :LANES]
    low = lax.broadcasted_iota(jnp.int32, (key_count, 128), 1) < 64
    middle = packed[:, 128:256]
    value = jnp.concatenate(
        [packed[:, 256:], jnp.where(low, jnp.ones_like(middle), middle)], axis=1
    )
    key_index = lax.broadcasted_iota(jnp.int32, (sparse, key_count), 1)
    query_index = lax.broadcasted_iota(jnp.int32, (sparse, key_count), 0) + where_ref[2]
    allowed = (key_index * RATE + phase < where_ref[1]) | (key_index == query_index)
    bias = jnp.where(allowed, 0.0, MASKED)
    near = near_ref[...]
    plain = jnp.zeros((row_count, LANES), jnp.float32)
    joined = jnp.zeros((sparse, LANES), jnp.float32)
    for head in range(PER_PHASE):
        own = jnp.where(key_lanes(head), query, jnp.zeros_like(query))
        scores = lax.dot_general(
            own, key, (((1,), (1,)), ((), ())), preferred_element_type=jnp.float32
        ) + bias
        top = jnp.max(scores, axis=1, keepdims=True)
        weights = jnp.exp2((scores - top) * EXP_SCALE)
        acc = fold_rows(weights.astype(jnp.bfloat16), value)
        total = acc[:, 128:129]
        near_total = near_own[:, 128 + head:129 + head]
        near_top = near_own[:, 132 + head:133 + head]
        best = jnp.maximum(top, near_top)
        near_coef = jnp.exp2((near_top - best) * EXP_SCALE)
        far_coef = jnp.exp2((top - best) * EXP_SCALE)
        merged = (near_coef * near_own + far_coef * acc) / (near_coef * near_total + far_coef * total)
        mine = value_lanes(head)
        joined = jnp.where(mine, merged, joined)
        plain = jnp.where(mine, near / near[:, 128 + head:129 + head], plain)
    att_ref[...] = plain.astype(jnp.bfloat16)
    for block, at in enumerate(starts):
        att_ref[pl.ds(at, PHASE_ROWS), :] = joined[
            block * PHASE_ROWS:(block + 1) * PHASE_ROWS
        ].astype(jnp.bfloat16)
    place = lax.broadcasted_iota(jnp.int32, (D, LANES), 0)
    spread = (place == value_src_ref[...]).astype(jnp.bfloat16)
    added = lax.dot_general(
        att_ref[...], spread, (((1,), (1,)), ((), ())), preferred_element_type=jnp.float32
    )

    @pl.when(phase == 0)
    def _():
        sum_ref[...] = added

    @pl.when(phase > 0)
    def _():
        sum_ref[...] += added

    @pl.when(phase == RATE - 1)
    def _():
        position = lax.broadcasted_iota(jnp.int32, (LOC, LOC), 0)
        row = lax.broadcasted_iota(jnp.int32, (LOC, LOC), 1)
        order = (row == (position & (RATE - 1)) * PHASE_ROWS + position // RATE).astype(jnp.bfloat16)
        for start in range(0, row_count, LOC):
            block = pl.ds(start, LOC)
            ordered = fold_rows(order, sum_ref[block, :].astype(jnp.bfloat16))
            live = lax.broadcasted_iota(jnp.int32, (LOC, 1), 0) + start < where_ref[0]
            out_ref[block, :] = jnp.where(live, ordered, 0.0).astype(jnp.bfloat16)


def attention(rows, place, query_weight, key_weight, value_weight, valid_limit, row_count):
    seg_count = lax.axis_size("seg")
    seg_here = lax.axis_index("seg")
    seg_tok = seg_count * row_count
    sparse = row_count // RATE
    seg_start = lax.axis_index("grp") * seg_tok
    where = jnp.stack([
        valid_limit - seg_start - seg_here * row_count,
        valid_limit - seg_start,
        seg_here * sparse,
    ]).astype(jnp.int32)
    key_src, value_src = (jnp.asarray(src) for src in lane_sources())
    wide = jax.ShapeDtypeStruct((row_count, RATE * LANES), jnp.bfloat16)
    params = pltpu.CompilerParams(vmem_limit_bytes=VMEM_LIMIT)
    whole = pl.BlockSpec(memory_space=pltpu.VMEM)
    scalars = pl.BlockSpec(memory_space=pltpu.SMEM)
    query, key, value, packed = pl.pallas_call(
        qkv_kernel,
        out_shape=(wide, wide, wide, jax.ShapeDtypeStruct((sparse, RATE * PACKED), jnp.bfloat16)),
        in_specs=[whole] * 7,
        out_specs=(whole,) * 4,
        compiler_params=params,
        name="qkv",
    )(rows, place, key_src, value_src, query_weight, key_weight, value_weight)
    shared = lax.all_gather(packed, "seg", axis=0)
    tile = pl.BlockSpec((LOC, LANES), lambda block, phase: (block, phase))
    near = pl.pallas_call(
        near_kernel,
        grid=(row_count // LOC, RATE),
        out_shape=jax.ShapeDtypeStruct((row_count, RATE * LANES), jnp.float32),
        in_specs=[scalars, tile, tile, tile],
        out_specs=tile,
        compiler_params=params,
        cost_estimate=pl.CostEstimate(
            flops=8 * row_count * LOC * HEADS * LANES // 2,
            bytes_accessed=20 * row_count * LANES,
            transcendentals=row_count * LOC * HEADS,
        ),
        name="near",
    )(where, query, key, value)
    tall = pl.BlockSpec((row_count, LANES), lambda phase: (0, phase))
    return pl.pallas_call(
        far_kernel,
        grid=(RATE,),
        out_shape=jax.ShapeDtypeStruct((row_count, D), jnp.bfloat16),
        in_specs=[
            scalars,
            pl.BlockSpec((1, LANES), lambda phase: (0, phase)),
            tall,
            tall,
            pl.BlockSpec((seg_count, sparse, PACKED), lambda phase: (0, 0, phase)),
        ],
        out_specs=pl.BlockSpec((row_count, D), lambda phase: (0, 0)),
        scratch_shapes=[
            pltpu.VMEM((row_count, LANES), jnp.bfloat16),
            pltpu.VMEM((row_count, D), jnp.float32),
        ],
        compiler_params=params,
        name="far",
    )(where, value_src, query, near, shared)


def feed_forward(tile_tokens, gate_weight, up_weight, down_weight, proj_weight):
    residual = tile_tokens.astype(jnp.float32)
    normed = layer_norm(residual, 1e-06).astype(jnp.bfloat16)
    gate_acc = fold_rows(normed, lax.all_gather(gate_weight, ("seg", "grp"), axis=0, tiled=True))
    up_acc = fold_rows(normed, lax.all_gather(up_weight, ("seg", "grp"), axis=0, tiled=True))
    hidden = (jax.nn.silu(gate_acc) * up_acc).astype(jnp.bfloat16)
    mixed = fold_rows(hidden, lax.all_gather(down_weight, ("seg", "grp"), axis=0, tiled=True))
    final_normed = layer_norm(residual + mixed, 1e-06).astype(jnp.bfloat16)
    return fold_rows(final_normed, proj_weight).astype(jnp.bfloat16)


def shards(
    tile_tokens,
    gate_weight,
    up_weight,
    down_weight,
    proj_weight,
    query_weight,
    key_weight,
    value_weight,
    tile_rank,
    valid_count,
):
    seg_count = lax.axis_size("seg")
    grp_count = lax.axis_size("grp")
    devices = seg_count * grp_count
    row_count = tile_tokens.shape[0]
    slot_cap = 2 * row_count // devices
    slots = devices * slot_cap
    seg_tok = seg_count * row_count
    target_grp = tile_rank // seg_tok
    target_seg = tile_rank % seg_tok // row_count
    target = target_seg * grp_count + target_grp
    within = tile_rank % row_count
    within = within // LOC * LOC + within % RATE * PHASE_ROWS + within % LOC // RATE
    onehot = target[:, None] == jnp.arange(devices, dtype=jnp.int32)[None, :]
    order = jnp.arange(row_count, dtype=jnp.int32)
    earlier = (order[None, :] < order[:, None]).astype(jnp.bfloat16)
    before = fold_rows(earlier, onehot.astype(jnp.bfloat16))
    rank_within = jnp.sum(jnp.where(onehot, before, 0.0), axis=1).astype(jnp.int32)
    slot_index = target * slot_cap + rank_within
    filled = jnp.arange(slots, dtype=jnp.int32)[:, None] == slot_index[None, :]
    send_place = jnp.sum(jnp.where(filled, within[None, :] + 1, 0), axis=1) - 1
    got_place = lax.all_to_all(
        send_place.reshape(devices, slot_cap),
        ("seg", "grp"),
        split_axis=0,
        concat_axis=0,
        tiled=True,
    ).reshape(1, slots)
    embedded = feed_forward(tile_tokens, gate_weight, up_weight, down_weight, proj_weight)
    send_rows = fold_rows(filled.astype(jnp.bfloat16), embedded).astype(jnp.bfloat16)
    got_rows = lax.all_to_all(
        send_rows.reshape(devices, slot_cap, D),
        ("seg", "grp"),
        split_axis=0,
        concat_axis=0,
        tiled=True,
    ).reshape(slots, D)
    attended = attention(
        got_rows, got_place, query_weight, key_weight, value_weight, valid_count[0], row_count
    )
    return attended[None]


def solution(mesh):
    return jax.shard_map(
        shards,
        mesh=mesh,
        in_specs=(
            P(("seg", "grp"), None),
            P(("seg", "grp"), None),
            P(("seg", "grp"), None),
            P(("seg", "grp"), None),
            P(),
            P(),
            P(),
            P(),
            P(("seg", "grp")),
            P(),
        ),
        out_specs=P("grp", "seg", None),
        check_vma=False,
    )
```

time: 734 us -> 424 us (0.58); the launches traced: 724 us -> 424 us
  local copies, waits for them, and re-layouts: 271 us -> 1.88 us
  matrix products: 105 us -> 47 us
  other arithmetic: 65.3 us -> 11.8 us
  Pallas kernels: 0 us -> 53.2 us
  waiting for transfers between devices: 254 us -> 285 us
    reshape x14 -> x1, local copies, waits for them, and re-layouts: 73 us -> 0.68 us  [shards(): got_place = lax.all_to_all(send_place.reshape(devices, slot_cap), ('seg',...]
    dot_general x16 -> x0, matrix products: 69.4 us -> none  [the longest x2 19.4 us: local_branch(): jnp.einsum('qhd,khd->hqk', query_blk, key_blk, preferred_element_type=jnp...]
    dynamic_update_slice x12 -> x0, local copies, waits for them, and re-layouts: 61.4 us -> none  [shards(): lax.map(local_branch, (query_rows.reshape(block_count, LOC, HEADS, head_s...]
    pallas_call x0 -> x3, Pallas kernels: none -> 53.2 us  [the longest x1 19.1 us: attention(): pl.pallas_call(qkv_kernel, out_shape=(wide, wide, wide, jax.ShapeDtypeStr...]
    all_gather x3 -> x4, waiting for transfers between devices: 177 us -> 212 us  [the longest x1 71 us: feed_forward(): lax.all_gather(up_weight, ('seg', 'grp'), axis=0, tiled=True)]
    mul x5 -> x0, local copies, waits for them, and re-layouts: 31 us -> none  [the longest x4 30.9 us: shards(): numerator = near_coef[..., None] * near_acc + far_coef[..., None] * far_acc]
    scatter x3 -> x0, local copies, waits for them, and re-layouts: 30.2 us -> none  [the longest x1 17.9 us: shards(): jnp.zeros((devices * slot_cap, D), jnp.bfloat16).at[slot_index]]
    reduce_sum x7 -> x1, other arithmetic: 24.5 us -> 0.92 us  [shards(): send_place = jnp.sum(jnp.where(filled, within[None, :] + 1, 0), axis=1) - 1]
  transfers between devices with their start and end apart: 8 -> 6, of which waited for: 5 -> 5; matrix products, arithmetic and copies ran while one was open for 38% -> 14% of each run, Pallas kernels for 0% -> 4%
where the time goes in v1:
time: 424 us
  waiting for transfers between devices  285 us (67%)
  Pallas kernels  53.2 us (13%)
  matrix products  47 us (11%)
  between operations  13.9 us (3%)
  other arithmetic  11.8 us (3%)
  starting transfers between devices  11.2 us (3%)
    all_gather x1, waiting for transfers between devices, feed_forward(): lax.all_gather(up_weight, ('seg', 'grp'), axis=0, tiled=True)  71 us
    all_to_all x1, waiting for transfers between devices, shards(): lax.all_to_all(send_rows.reshape(devices, slot_cap, D), ('seg', 'grp'), s...  70.5 us
    all_gather x1, waiting for transfers between devices, feed_forward(): lax.all_gather(down_weight, ('seg', 'grp'), axis=0, tiled=True)  58.6 us
    all_gather x1, waiting for transfers between devices, feed_forward(): lax.all_gather(gate_weight, ('seg', 'grp'), axis=0, tiled=True)  58.3 us
    dot_general x4, matrix products, fold_rows(): return jnp.dot(left, piece, preferred_element_type=jnp.float32)  47 us
    all_gather x1, waiting for transfers between devices, attention(): shared = lax.all_gather(packed, 'seg', axis=0)  24.6 us
    pallas_call x1, Pallas kernels, attention(): pl.pallas_call(qkv_kernel, out_shape=(wide, wide, wide, jax.ShapeDtypeStr...  19.1 us
    pallas_call x1, Pallas kernels, attention(): pl.pallas_call(far_kernel, grid=(RATE,), out_shape=jax.ShapeDtypeStruct((...  18.4 us
  transfers between devices with their start and end apart: 6, of which 5 were waited for; matrix products, arithmetic and copies ran while one was open for 14% of the time, Pallas kernels for 4%

profile of v1, /device:TPU:0, one launch (start us, length us, event | category | flops | bytes accessed | tf_op | source)
XLA Modules:
  0.0 424.0 jit_solution(4334551291805250160)
XLA Ops:
  6.5 0.7 all-gather.6.cloned.1.call-update
  7.3 0.7 all-gather.10.cloned.1.call-update
  8.1 0.7 all-gather.8.cloned.1.call-update
  8.7 0.7 fusion.21
  10.0 0.9 select_reduce_fusion
  10.9 0.7 sub.58
  11.6 7.3 %all-to-all-start.1 = ((s32[32,1,64]{2,1,0:T(1,128)}), s32[32,1,64]{2,1,0:T(1,128)S(1)}, u32[]{:S(2)}, u32[]{:S(2)}) async-start(s32[32,1,64]{2,1,0:T(1,128)} %sub.58), calls=%async_computation.1 | async-start | bytes 32768 | tf_op jit(solution)/shard_map/all_to_all | solution.py:293
  18.9 2.4 convert_reduce_fusion
  21.3 2.9 fusion.3
  24.3 58.3 %all-gather.6.cloned.1.call-done = bf16[1536,2048]{1,0:T(8,128)(2,1)} async-done(((bf16[48,2048]{1,0:T(8,128)(2,1)}), bf16[1536,2048]{1,0:T(8,128)(2,1)}) %all-gather.6.cloned.1.call-update) | async-done | bytes 6291472 | tf_op jit(solution)/shard_map/all_gather | solution.py:253
  82.6 12.4 %fusion.32 = f32[1024,2048]{1,0:T(8,128)} fusion(bf16[1536,2048]{1,0:T(8,128)(2,1)} %all-gather.6.cloned.1.call-done, bf16[1024,1536]{1,0:T(8,128)(2,1)} %param.12, f32[1024]{0:T(1024)S(1)} %add_rsqrt_fusion.1, f32[1024]{0:T(1024)S(1)} %broadcast_multiply_fusion.1), kind=kOutput, calls=%fused_computation.74 | convolution fusion | flops 6448742400 | bytes 17833984 | tf_op jit(solution)/shard_map/dot_general | solution.py:33
  95.0 58.6 %all-gather.10.cloned.1.call-done = bf16[2048,1536]{1,0:T(8,128)(2,1)} async-done(((bf16[64,1536]{1,0:T(8,128)(2,1)}), bf16[2048,1536]{1,0:T(8,128)(2,1)}) %all-gather.10.cloned.1.call-update) | async-done | bytes 6291472 | tf_op jit(solution)/shard_map/all_gather | solution.py:256
  153.6 71.0 %all-gather.8.cloned.1.call-done = bf16[1536,2048]{1,0:T(8,128)(2,1)} async-done(((bf16[48,2048]{1,0:T(8,128)(2,1)}), bf16[1536,2048]{1,0:T(8,128)(2,1)}) %all-gather.8.cloned.1.call-update) | async-done | bytes 6291472 | tf_op jit(solution)/shard_map/all_gather | solution.py:254
  224.5 23.5 %fusion.34 = (f32[1024]{0:T(1024)S(1)}, f32[1024,1536]{1,0:T(8,128)}) fusion(bf16[2048,1536]{1,0:T(8,128)(2,1)} %all-gather.10.cloned.1.call-done, bf16[1024,1536]{1,0:T(8,128)(2,1)} %param.12, f32[1024,2048]{1,0:T(8,128)} %fusion.32, bf16[1536,2048]{1,0:T(8,128)(2,1)} %all-gather.8.cloned.1.call-done, f32[1024]{0:T(1024)S(1)} %add_rsqrt_fusion.1, ...), kind=kOutput, calls=%fused_computation.75 | convolution fusion | flops 12908493824 | bytes 30420992 | tf_op jit(solution)/shard_map/dot_general | solution.py:33
  248.0 3.5 multiply_reduce_fusion
  251.6 10.6 %fusion.7 = bf16[2048,768]{1,0:T(8,128)(2,1)} fusion(s32[1024]{0:T(1024)S(1)} %convert_add_fusion.1, bf16[1536,768]{1,0:T(8,128)(2,1)S(1)} %copy-done, f32[1024,1536]{1,0:T(8,128)} %get-tuple-element.16, f32[1024]{0:T(1024)S(1)} %add_rsqrt_fusion, f32[1024]{0:T(1024)S(1)} %broadcast_multiply_fusion), kind=kOutput, calls=%fused_computation.16 | convolution fusion | flops 5646319616 | bytes 11808768 | tf_op jit(solution)/shard_map/dot_general | solution.py:33
  262.2 3.5 all-to-all-start
  266.5 0.7 reduce.3
  267.2 0.7 reshape.56.place_ref
  267.9 70.5 %all-to-all-done = bf16[32,64,768]{2,1,0:T(8,128)(2,1)} async-done(((bf16[32,64,768]{2,1,0:T(8,128)(2,1)}), bf16[32,64,768]{2,1,0:T(8,128)(2,1)}, u32[]{:S(2)}, u32[]{:S(2)}) %all-to-all-start) | async-done | bytes 3145760 | tf_op jit(solution)/shard_map/all_to_all | solution.py:302
  338.4 19.1 %qkv.1 = (bf16[1024,1024]{1,0:T(8,128)(2,1)}, bf16[1024,1024]{1,0:T(8,128)(2,1)}, bf16[1024,1024]{1,0:T(8,128)(2,1)}, bf16[256,1536]{1,0:T(8,128)(2,1)}) custom-call(bf16[2048,768]{1,0:T(8,128)(2,1)} %bitcast.5.rows_ref, s32[1,2048]{1,0:T(1,128)} %reshape.56.place_ref, s32[1,1024]{1,0:T(1,128)} %constant.126.clone.key_src_ref, ...), custom_call_target="tpu_custom_call" | custom-call | tf_op jit(solution)/shard_map/qkv/pallas_call | solution.py:204
  358.7 15.8 %near.1.near_ref = f32[1024,1024]{1,0:T(8,128)} custom-call(s32[3]{0:T(128)} %pad_add_fusion.where_ref, bf16[1024,1024]{1,0:T(8,128)(2,1)} %get-tuple-element.9.q_ref, bf16[1024,1024]{1,0:T(8,128)(2,1)} %get-tuple-element.10.k_ref, bf16[1024,1024]{1,0:T(8,128)(2,1)} %get-tuple-element.11.v_ref), custom_call_target="tpu_custom_call" | custom-call | flops 8589934592 | bytes 5242880 | tf_op jit(solution)/shard_map/near/pallas_call | solution.py:214
  374.5 24.6 %all-gather.12.cloned.1.call-done = bf16[1024,1536]{1,0:T(8,128)(2,1)} async-done(((bf16[256,1536]{1,0:T(8,128)(2,1)}), bf16[1024,1536]{1,0:T(8,128)(2,1)}) %all-gather.12.cloned.1.call-update) | async-done | bytes 3145744 | tf_op jit(solution)/shard_map/all_gather | solution.py:212
  399.1 18.4 %far.1 = bf16[1024,768]{1,0:T(8,128)(2,1)} custom-call(s32[3]{0:T(128)} %pad_add_fusion.where_ref, s32[1,1024]{1,0:T(1,128)} %constant.127.clone.value_src_ref, bf16[1024,1024]{1,0:T(8,128)(2,1)} %get-tuple-element.9.q_ref, f32[1024,1024]{1,0:T(8,128)} %near.1.near_ref, bf16[4,256,1536]{2,1,0:T(8,128)(2,1)} %bitcast.19), custom_call_target="tpu_custom_call" | custom-call | tf_op jit(solution)/shard_map/far/pallas_call | solution.py:229
  (17 shorter events, 2.0 us)
Async XLA Ops:
  6.5 245.0 %copy-start = (bf16[1536,768]{1,0:T(8,128)(2,1)S(1)}, bf16[1536,768]{1,0:T(8,128)(2,1)}, u32[]{:S(2)}) copy-start(bf16[1536,768]{1,0:T(8,128)(2,1)} %param.16) | copy-start | bytes 7077892
  6.5 76.1 %all-gather.6.cloned.1.call-start = ((), (), s32[]{:S(2)}) async-start(), calls=%async_computation.2 | async-start | bytes 6488064 | tf_op jit(solution)/shard_map/all_gather | solution.py:253
  7.3 146.3 %all-gather.10.cloned.1.call-start = ((), (), s32[]{:S(2)}) async-start(), calls=%async_computation.4 | async-start | bytes 6488064 | tf_op jit(solution)/shard_map/all_gather | solution.py:256
  8.0 216.5 %all-gather.8.cloned.1.call-start = ((), (), s32[]{:S(2)}) async-start(), calls=%async_computation.3 | async-start | bytes 6488064 | tf_op jit(solution)/shard_map/all_gather | solution.py:254
  11.6 250.6 %all-to-all-start.1 = ((s32[32,1,64]{2,1,0:T(1,128)}), s32[32,1,64]{2,1,0:T(1,128)S(1)}, u32[]{:S(2)}, u32[]{:S(2)}) async-start(s32[32,1,64]{2,1,0:T(1,128)} %sub.58), calls=%async_computation.1 | async-start | bytes 32768 | tf_op jit(solution)/shard_map/all_to_all | solution.py:293
  262.2 76.2 %all-to-all-start = ((bf16[32,64,768]{2,1,0:T(8,128)(2,1)}), bf16[32,64,768]{2,1,0:T(8,128)(2,1)}, u32[]{:S(2)}, u32[]{:S(2)}) async-start(bf16[32,64,768]{2,1,0:T(8,128)(2,1)} %bitcast.18), calls=%async_computation | async-start | bytes 6291456 | tf_op jit(solution)/shard_map/all_to_all | solution.py:302
  265.7 133.3 %all-gather.12.cloned.1.call-start = ((), (), s32[]{:S(2)}) async-start(), calls=%async_computation.5 | async-start | bytes 3932160 | tf_op jit(solution)/shard_map/all_gather | solution.py:212
Sparse Core Ops, SparseCore 0:
  10.4 72.1 all-gather.5
  85.6 67.9 all-gather.9
  156.6 67.9 all-gather.7
  357.6 41.4 all-gather.11

commit v2 on v1

--- a/solution.py
+++ b/solution.py
@@ -19,6 +19,8 @@
 PHASE_ROWS = LOC // RATE
 EXP_SCALE = math.log2(math.e) / math.sqrt(HEAD)
 MASKED = -1e30
+ROW_TILE = 256
+COLUMN_TILE = 512
 VMEM_LIMIT = 56 * 1024 * 1024
 
 
@@ -247,6 +249,235 @@
     )(where, value_src, query, near, shared)
 
 
+def block_half(ref, rows, half):
+    if half is None:
+        return ref.at[rows, :]
+    width = ref.shape[1] // 2
+    return ref.at[rows, half * width:(half + 1) * width]
+
+
+def expert_kernel(
+    tokens_ref, gate_ref, up_ref, down_ref, proj_ref, slot_ref, out_ref,
+    wide_ref, deep_ref, normed_ref, hidden_ref, embedded_ref, send_sem, recv_sem,
+):
+    seg, grp = lax.axis_index("seg"), lax.axis_index("grp")
+    core, z = grp % 2, grp // 2
+    seg_x = seg // 2 * 2 + 1 - seg % 2
+    seg_y = (seg + 2) % 4
+    seg_d = seg_y // 2 * 2 + 1 - seg_y % 2
+    sibling = z * 2 + 1 - core
+    gathered = (wide_ref, deep_ref)
+    depth = (gate_ref.shape[0], down_ref.shape[0])
+    copies = {
+        "up": (0, (seg, grp + 2), None),
+        "down": (9, (seg, grp - 2), None),
+        "x": (1, (seg_x, grp), None),
+        "y": (2, (seg_y, grp), None),
+        "xy": (3, (seg_y, grp), 0),
+        "yx": (4, (seg_x, grp), 1),
+        "own": (5, (seg, sibling), None),
+        "own_x": (6, (seg, sibling), None),
+        "own_y": (7, (seg, sibling), None),
+        "own_d": (8, (seg, sibling), None),
+    }
+    sent_block = {
+        "up": seg, "down": seg, "x": seg, "y": seg, "xy": seg_x, "yx": seg_y,
+        "own": seg, "own_x": seg_x, "own_y": seg_y, "own_d": seg_d,
+    }
+    got_block = {
+        "up": seg, "x": seg_x, "y": seg_y, "xy": seg_d, "yx": seg_d,
+        "own": seg, "own_x": seg_x, "own_y": seg_y, "own_d": seg_d,
+    }
+
+    def rows_of(which, block_seg, j, block_core):
+        owner = block_seg * 8 + j * 2 + block_core
+        return pl.ds(pl.multiple_of(owner * depth[which], 16), depth[which])
+
+    def outgoing(which, j, kind):
+        index, target, half = copies[kind]
+        block = block_half(gathered[which], rows_of(which, sent_block[kind], j, core), half)
+        return pltpu.make_async_remote_copy(
+            src_ref=block,
+            dst_ref=block,
+            send_sem=send_sem.at[which, j, index],
+            recv_sem=recv_sem.at[which, j, 0 if kind == "down" else index],
+            device_id=target,
+            device_id_type=pl.DeviceIdType.MESH,
+        )
+
+    def arrived(which, j, kind):
+        index, target, half = copies[kind]
+        from_core = 1 - core if kind.startswith("own") else core
+        block = block_half(gathered[which], rows_of(which, got_block[kind], j, from_core), half)
+        pltpu.make_async_remote_copy(
+            src_ref=block,
+            dst_ref=block,
+            send_sem=send_sem.at[which, j, index],
+            recv_sem=recv_sem.at[which, j, index],
+            device_id=(seg, sibling),
+            device_id_type=pl.DeviceIdType.MESH,
+        ).wait_recv()
+
+    def each_of_wave(k, do):
+        if k == 0:
+            do(z, True, True)
+        else:
+            pl.when(z >= k)(lambda: do(z - k, True, False))
+            pl.when(z + k <= 3)(lambda: do(z + k, False, True))
+
+    def enter(which, k):
+        def do(j, rising, falling):
+            if k > 0:
+                arrived(which, j, "up")
+            if rising:
+                pl.when(z < 3)(lambda: outgoing(which, j, "up").start())
+            if falling:
+                pl.when(z > 0)(lambda: outgoing(which, j, "down").start())
+            for kind in ("x", "y", "own"):
+                outgoing(which, j, kind).start()
+        each_of_wave(k, do)
+
+    def cross(which, k):
+        def do(j, rising, falling):
+            arrived(which, j, "x")
+            outgoing(which, j, "xy").start()
+            outgoing(which, j, "own_x").start()
+            arrived(which, j, "y")
+            outgoing(which, j, "yx").start()
+            outgoing(which, j, "own_y").start()
+        each_of_wave(k, do)
+
+    def close(which, k):
+        def do(j, rising, falling):
+            arrived(which, j, "xy")
+            arrived(which, j, "yx")
+            outgoing(which, j, "own_d").start()
+        each_of_wave(k, do)
+
+    def advance(which, step):
+        if 0 <= step < 4:
+            enter(which, step)
+        if 0 <= step - 1 < 4:
+            cross(which, step - 1)
+        if 0 <= step - 2 < 4:
+            close(which, step - 2)
+
+    def from_sibling(which):
+        for j in range(4):
+            for kind in ("own", "own_x", "own_y", "own_d"):
+                arrived(which, j, kind)
+
+    barrier = pltpu.get_barrier_semaphore()
+
+    def greet(target):
+        pl.semaphore_signal(
+            barrier, inc=1, device_id=target, device_id_type=pl.DeviceIdType.MESH
+        )
+
+    for target in ((seg_x, grp), (seg_y, grp), (seg, sibling)):
+        greet(target)
+    pl.when(z < 3)(lambda: greet((seg, grp + 2)))
+    pl.when(z > 0)(lambda: greet((seg, grp - 2)))
+    pl.semaphore_wait(barrier, 4 + (z + 1) // 2 % 2)
+
+    half_width = gate_ref.shape[1]
+    wide_ref[rows_of(0, seg, z, core), :half_width] = gate_ref[...]
+    wide_ref[rows_of(0, seg, z, core), half_width:] = up_ref[...]
+    deep_ref[rows_of(1, seg, z, core), :] = down_ref[...]
+    advance(0, 0)
+
+    row_count = tokens_ref.shape[0]
+
+    @pl.loop(0, row_count // ROW_TILE)
+    def _(tile):
+        rows = pl.ds(pl.multiple_of(tile * ROW_TILE, ROW_TILE), ROW_TILE)
+        normed_ref[rows, :] = layer_norm(
+            tokens_ref[rows, :].astype(jnp.float32), 1e-06
+        ).astype(jnp.bfloat16)
+
+    for step in range(1, 6):
+        advance(0, step)
+        advance(1, step - 3)
+    from_sibling(0)
+
+    def gate_up(tile):
+        rows = pl.ds(tile * ROW_TILE, ROW_TILE)
+
+        @pl.loop(0, half_width // COLUMN_TILE)
+        def _(part):
+            at = pl.multiple_of(part * COLUMN_TILE, COLUMN_TILE)
+            past = pl.multiple_of(part * COLUMN_TILE + half_width, COLUMN_TILE)
+            normed = normed_ref[rows, :]
+            gate = fold_rows(normed, wide_ref[:, pl.ds(at, COLUMN_TILE)])
+            up = fold_rows(normed, wide_ref[:, pl.ds(past, COLUMN_TILE)])
+            hidden_ref[rows, pl.ds(at, COLUMN_TILE)] = (
+                gate / (1.0 + jnp.exp(-gate)) * up
+            ).astype(jnp.bfloat16)
+
+    tiles = row_count // ROW_TILE
+    gate_up(0)
+    for step in range(6, 9):
+        advance(1, step - 3)
+        if step - 5 < tiles:
+            gate_up(step - 5)
+    for tile in range(4, tiles):
+        gate_up(tile)
+    from_sibling(1)
+
+    @pl.loop(0, tiles)
+    def _(tile):
+        rows = pl.ds(pl.multiple_of(tile * ROW_TILE, ROW_TILE), ROW_TILE)
+        mixed = tokens_ref[rows, :].astype(jnp.float32) + fold_rows(
+            hidden_ref[rows, :], deep_ref[...]
+        )
+        final = layer_norm(mixed, 1e-06).astype(jnp.bfloat16)
+        embedded_ref[rows, :] = fold_rows(final, proj_ref[...]).astype(jnp.bfloat16)
+
+    @pl.loop(0, out_ref.shape[0] // ROW_TILE)
+    def _(tile):
+        start = pl.multiple_of(tile * ROW_TILE, ROW_TILE)
+        slot = lax.broadcasted_iota(jnp.int32, (ROW_TILE, row_count), 0) + start
+        pick = (slot == slot_ref[...]).astype(jnp.bfloat16)
+        out_ref[pl.ds(start, ROW_TILE), :] = fold_rows(pick, embedded_ref[...]).astype(jnp.bfloat16)
+
+    for which in range(2):
+        for j in range(4):
+            for kind in copies:
+                if kind == "up":
+                    pl.when((z < 3) & (z >= j))(lambda: outgoing(which, j, "up").wait_send())
+                elif kind == "down":
+                    pl.when((z > 0) & (z <= j))(lambda: outgoing(which, j, "down").wait_send())
+                else:
+                    outgoing(which, j, kind).wait_send()
+
+
+def gathered_send_rows(
+    tile_tokens, gate_weight, up_weight, down_weight, proj_weight, slot_index, slots
+):
+    row_count, width = tile_tokens.shape
+    hidden_width = gate_weight.shape[1]
+    whole = pl.BlockSpec(memory_space=pltpu.VMEM)
+    return pl.pallas_call(
+        expert_kernel,
+        out_shape=jax.ShapeDtypeStruct((slots, D), jnp.bfloat16),
+        in_specs=[whole] * 6,
+        out_specs=whole,
+        scratch_shapes=[
+            pltpu.VMEM((width, 2 * hidden_width), jnp.bfloat16),
+            pltpu.VMEM((hidden_width, width), jnp.bfloat16),
+            pltpu.VMEM((row_count, width), jnp.bfloat16),
+            pltpu.VMEM((row_count, hidden_width), jnp.bfloat16),
+            pltpu.VMEM((row_count, D), jnp.bfloat16),
+            pltpu.SemaphoreType.DMA((2, 4, 10)),
+            pltpu.SemaphoreType.DMA((2, 4, 9)),
+        ],
+        compiler_params=pltpu.CompilerParams(
+            collective_id=0, has_side_effects=True, vmem_limit_bytes=VMEM_LIMIT
+        ),
+        name="feed_forward",
+    )(tile_tokens, gate_weight, up_weight, down_weight, proj_weight, slot_index.reshape(1, -1))
+
+
 def feed_forward(tile_tokens, gate_weight, up_weight, down_weight, proj_weight):
     residual = tile_tokens.astype(jnp.float32)
     normed = layer_norm(residual, 1e-06).astype(jnp.bfloat16)
@@ -297,8 +528,13 @@
         concat_axis=0,
         tiled=True,
     ).reshape(1, slots)
-    embedded = feed_forward(tile_tokens, gate_weight, up_weight, down_weight, proj_weight)
-    send_rows = fold_rows(filled.astype(jnp.bfloat16), embedded).astype(jnp.bfloat16)
+    if (seg_count, grp_count) == (4, 8):
+        send_rows = gathered_send_rows(
+            tile_tokens, gate_weight, up_weight, down_weight, proj_weight, slot_index, slots
+        )
+    else:
+        embedded = feed_forward(tile_tokens, gate_weight, up_weight, down_weight, proj_weight)
+        send_rows = fold_rows(filled.astype(jnp.bfloat16), embedded).astype(jnp.bfloat16)
     got_rows = lax.all_to_all(
         send_rows.reshape(devices, slot_cap, D),
         ("seg", "grp"),

time: 424 us -> 296 us (0.70)
  waiting for transfers between devices: 285 us -> 95.2 us
  Pallas kernels: 53.2 us -> 165 us
  matrix products: 47 us -> 0.53 us
  other arithmetic: 11.8 us -> 2.94 us
    all_gather x3 -> x0, waiting for transfers between devices: 188 us -> none  [the longest x1 71 us: feed_forward(): lax.all_gather(up_weight, ('seg', 'grp'), axis=0, tiled=True)]
    pallas_call x0 -> x1, Pallas kernels: none -> 112 us  [gathered_send_rows(): pl.pallas_call(expert_kernel, out_shape=jax.ShapeDtypeStruct((slots, D),...]
    dot_general x4 -> x1, matrix products: 47 us -> 0.53 us  [fold_rows(): return jnp.dot(left, piece, preferred_element_type=jnp.float32)]
    reduce_sum x3 -> x0, other arithmetic: 8.84 us -> none  [the longest x2 6.46 us: layer_norm(): row_var = jnp.mean(centered * centered, axis=-1, keepdims=True)]
  transfers between devices with their start and end apart: 6 -> 3, of which waited for: 5 -> 2; matrix products, arithmetic and copies ran while one was open for 14% -> 1% of each run, Pallas kernels for 4% -> 43%
where the time goes in v2:
time: 296 us
  Pallas kernels  165 us (56%)
  waiting for transfers between devices  95.2 us (32%)
  starting transfers between devices  14.4 us (5%)
  between operations  14.1 us (5%)
  local copies, waits for them, and re-layouts  3.53 us (1%)
    pallas_call x1, Pallas kernels, gathered_send_rows(): pl.pallas_call(expert_kernel, out_shape=jax.ShapeDtypeStruct((slots, D),...  112 us
    all_to_all x1, waiting for transfers between devices, shards(): lax.all_to_all(send_rows.reshape(devices, slot_cap, D), ('seg', 'grp'), s...  70.5 us
    all_gather x1, waiting for transfers between devices, attention(): shared = lax.all_gather(packed, 'seg', axis=0)  24.7 us
    pallas_call x1, Pallas kernels, attention(): pl.pallas_call(qkv_kernel, out_shape=(wide, wide, wide, jax.ShapeDtypeStr...  19 us
    pallas_call x1, Pallas kernels, attention(): pl.pallas_call(far_kernel, grid=(RATE,), out_shape=jax.ShapeDtypeStruct((...  18.4 us
    pallas_call x1, Pallas kernels, attention(): pl.pallas_call(near_kernel, grid=(row_count // LOC, RATE), out_shape=jax....  15.7 us
    all_to_all x1, starting transfers between devices, shards(): lax.all_to_all(send_place.reshape(devices, slot_cap), ('seg', 'grp'), spl...  7.3 us
    all_to_all x1, starting transfers between devices, shards(): lax.all_to_all(send_rows.reshape(devices, slot_cap, D), ('seg', 'grp'), s...  6.85 us
  transfers between devices with their start and end apart: 3, of which 2 were waited for; matrix products, arithmetic and copies ran while one was open for 1% of the time, Pallas kernels for 43%

profile of v2, /device:TPU:0, one launch (start us, length us, event | category | flops | bytes accessed | tf_op | source)
XLA Modules:
  0.0 295.8 jit_solution(14688864378411148868)
XLA Ops:
  6.5 0.7 fusion.10
  7.2 0.5 fusion.2
  7.8 0.0 copy-start.1
  7.8 0.9 select_reduce_fusion
  8.7 0.7 sub.38
  9.4 7.3 %all-to-all-start.1 = ((s32[32,1,64]{2,1,0:T(1,128)}), s32[32,1,64]{2,1,0:T(1,128)S(1)}, u32[]{:S(2)}, u32[]{:S(2)}) async-start(s32[32,1,64]{2,1,0:T(1,128)} %sub.38), calls=%async_computation.1 | async-start | bytes 32768 | tf_op jit(solution)/shard_map/all_to_all | solution.py:524
  16.7 0.0 copy-done.1
  16.8 111.9 %feed_forward.1 = bf16[2048,768]{1,0:T(8,128)(2,1)} custom-call(bf16[1024,1536]{1,0:T(8,128)(2,1)} %tokens_ref.1, bf16[48,2048]{1,0:T(8,128)(2,1)} %gate_ref.1, bf16[48,2048]{1,0:T(8,128)(2,1)} %up_ref.1, bf16[64,1536]{1,0:T(8,128)(2,1)} %down_ref.1, bf16[1536,768]{1,0:T(8,128)(2,1)} %proj_ref.1, s32[1,1024]{1,0:T(1,128)} %bitcast.13), custom_call_target="tpu_custom_call" | custom-call | tf_op jit(solution)/shard_map/feed_forward/pallas_call | solution.py:460
  128.6 0.0 all-to-all-done.1
  128.7 6.8 %all-to-all-start = ((bf16[32,64,768]{2,1,0:T(8,128)(2,1)}), bf16[32,64,768]{2,1,0:T(8,128)(2,1)S(1)}, u32[]{:S(2)}, u32[]{:S(2)}) async-start(bf16[32,64,768]{2,1,0:T(8,128)(2,1)} %bitcast.11), calls=%async_computation | async-start | bytes 6291456 | tf_op jit(solution)/shard_map/all_to_all | solution.py:538
  135.5 0.2 all-gather.3.cloned.1.call-start
  135.7 0.5 broadcast.65
  136.3 0.7 reduce.3
  136.9 0.7 reshape.36.place_ref
  137.6 70.5 %all-to-all-done = bf16[32,64,768]{2,1,0:T(8,128)(2,1)S(1)} async-done(((bf16[32,64,768]{2,1,0:T(8,128)(2,1)}), bf16[32,64,768]{2,1,0:T(8,128)(2,1)S(1)}, u32[]{:S(2)}, u32[]{:S(2)}) %all-to-all-start) | async-done | bytes 3145760 | tf_op jit(solution)/shard_map/all_to_all | solution.py:538
  208.1 0.0 copy-start
  208.1 1.6 copy-done
  209.8 19.0 %qkv.1 = (bf16[1024,1024]{1,0:T(8,128)(2,1)}, bf16[1024,1024]{1,0:T(8,128)(2,1)}, bf16[1024,1024]{1,0:T(8,128)(2,1)}, bf16[256,1536]{1,0:T(8,128)(2,1)}) custom-call(bf16[2048,768]{1,0:T(8,128)(2,1)} %bitcast.10, s32[1,2048]{1,0:T(1,128)} %reshape.36.place_ref, s32[1,1024]{1,0:T(1,128)} %constant.115.clone.key_src_ref, ...), custom_call_target="tpu_custom_call" | custom-call | tf_op jit(solution)/shard_map/qkv/pallas_call | solution.py:206
  228.8 0.0 all-gather.3.cloned.1.call-update
  229.5 0.6 pad_add_fusion.where_ref
  230.1 15.7 %near.1.near_ref = f32[1024,1024]{1,0:T(8,128)} custom-call(s32[3]{0:T(128)} %pad_add_fusion.where_ref, bf16[1024,1024]{1,0:T(8,128)(2,1)} %get-tuple-element.9.q_ref, bf16[1024,1024]{1,0:T(8,128)(2,1)} %get-tuple-element.10.k_ref, bf16[1024,1024]{1,0:T(8,128)(2,1)} %get-tuple-element.11.v_ref), custom_call_target="tpu_custom_call" | custom-call | flops 8589934592 | bytes 5242880 | tf_op jit(solution)/shard_map/near/pallas_call | solution.py:216
  245.9 24.7 %all-gather.3.cloned.1.call-done = bf16[1024,1536]{1,0:T(8,128)(2,1)} async-done(((bf16[256,1536]{1,0:T(8,128)(2,1)}), bf16[1024,1536]{1,0:T(8,128)(2,1)}) %all-gather.3.cloned.1.call-update) | async-done | bytes 3145744 | tf_op jit(solution)/shard_map/all_gather | solution.py:214
  270.6 18.4 %far.1 = bf16[1024,768]{1,0:T(8,128)(2,1)} custom-call(s32[3]{0:T(128)} %pad_add_fusion.where_ref, s32[1,1024]{1,0:T(1,128)} %constant.116.clone.value_src_ref, bf16[1024,1024]{1,0:T(8,128)(2,1)} %get-tuple-element.9.q_ref, f32[1024,1024]{1,0:T(8,128)} %near.1.near_ref, bf16[4,256,1536]{2,1,0:T(8,128)(2,1)} %bitcast.12), custom_call_target="tpu_custom_call" | custom-call | tf_op jit(solution)/shard_map/far/pallas_call | solution.py:231
  (2 shorter events, 0.0 us)
Async XLA Ops:
  7.8 8.9 %copy-start.1 = (s32[1024]{0:T(1024)}, s32[1024]{0:T(1024)S(1)}, u32[]{:S(2)}) copy-start(s32[1024]{0:T(1024)S(1)} %convert_add_fusion) | copy-start | bytes 12292
  9.4 119.2 %all-to-all-start.1 = ((s32[32,1,64]{2,1,0:T(1,128)}), s32[32,1,64]{2,1,0:T(1,128)S(1)}, u32[]{:S(2)}, u32[]{:S(2)}) async-start(s32[32,1,64]{2,1,0:T(1,128)} %sub.38), calls=%async_computation.1 | async-start | bytes 32768 | tf_op jit(solution)/shard_map/all_to_all | solution.py:524
  128.7 79.5 %all-to-all-start = ((bf16[32,64,768]{2,1,0:T(8,128)(2,1)}), bf16[32,64,768]{2,1,0:T(8,128)(2,1)S(1)}, u32[]{:S(2)}, u32[]{:S(2)}) async-start(bf16[32,64,768]{2,1,0:T(8,128)(2,1)} %bitcast.11), calls=%async_computation | async-start | bytes 6291456 | tf_op jit(solution)/shard_map/all_to_all | solution.py:538
  135.5 135.1 %all-gather.3.cloned.1.call-start = ((), (), s32[]{:S(2)}) async-start(), calls=%async_computation.2 | async-start | bytes 3932160 | tf_op jit(solution)/shard_map/all_gather | solution.py:214
  208.1 1.7 copy-start
Sparse Core Ops, SparseCore 0:
  229.0 41.5 all-gather.2

commit v3 on v2

--- a/solution.py
+++ b/solution.py
@@ -57,49 +57,57 @@
     return (dim >= head * HEAD) & (dim < (head + 1) * HEAD)
 
 
-def qkv_kernel(
-    rows_ref, place_ref, key_src_ref, value_src_ref, wq_ref, wk_ref, wv_ref,
-    q_ref, k_ref, v_ref, kv_ref,
-):
-    row_count = q_ref.shape[0]
+def pick_weights_kernel(key_src_ref, value_src_ref, wq_ref, wk_ref, wv_ref, q_ref, k_ref, v_ref):
     column = lax.broadcasted_iota(jnp.int32, (D, RATE * LANES), 0)
     pick_key = (column == key_src_ref[...]).astype(jnp.bfloat16)
     pick_value = (column == value_src_ref[...]).astype(jnp.bfloat16)
-    wq = fold_rows(wq_ref[...], pick_key).astype(jnp.bfloat16)
-    wk = fold_rows(wk_ref[...], pick_key).astype(jnp.bfloat16)
-    wv = fold_rows(wv_ref[...], pick_value).astype(jnp.bfloat16)
+    q_ref[...] = fold_rows(wq_ref[...], pick_key).astype(jnp.bfloat16)
+    k_ref[...] = fold_rows(wk_ref[...], pick_key).astype(jnp.bfloat16)
+    v_ref[...] = fold_rows(wv_ref[...], pick_value).astype(jnp.bfloat16)
+
+
+def key_value_block(start, rows_ref, place_ref, value_src_ref, wk_ref, wv_ref, normed_ref, k_ref, v_ref, kv_ref, kv_start):
     place = place_ref[...]
-    spare = value_src_ref[...] < 0
-    for start in range(0, row_count, LOC):
-        here = lax.broadcasted_iota(jnp.int32, (LOC, place.shape[1]), 0) + start
-        pick = (here == place).astype(jnp.bfloat16)
-        seq = fold_rows(pick, rows_ref[...])
-        normed = layer_norm(seq, 1e-05).astype(jnp.bfloat16)
+    here = lax.broadcasted_iota(jnp.int32, (LOC, place.shape[1]), 0) + start
+    pick = (here == place).astype(jnp.bfloat16)
+    seq = fold_rows(pick, rows_ref[...])
+    normed = layer_norm(seq, 1e-05).astype(jnp.bfloat16)
+    block = pl.ds(start, LOC)
+    normed_ref[block, :] = normed
+    key = fold_rows(normed, wk_ref[...]).astype(jnp.bfloat16)
+    value = jnp.where(value_src_ref[...] < 0, 1.0, fold_rows(normed, wv_ref[...])).astype(jnp.bfloat16)
+    k_ref[block, :] = key
+    v_ref[block, :] = value
+    low = lax.broadcasted_iota(jnp.int32, (PHASE_ROWS, 128), 1) < 64
+    out = pl.ds(pl.multiple_of(kv_start + start // RATE, PHASE_ROWS), PHASE_ROWS)
+    for phase in range(RATE):
+        kp = key[phase * PHASE_ROWS:(phase + 1) * PHASE_ROWS, phase * LANES:(phase + 1) * LANES]
+        vp = value[phase * PHASE_ROWS:(phase + 1) * PHASE_ROWS, phase * LANES:(phase + 1) * LANES]
+        at = phase * PACKED
+        kv_ref[out, at:at + 128] = kp[:, :128]
+        kv_ref[out, at + 128:at + 256] = jnp.where(low, kp[:, 128:], vp[:, 128:])
+        kv_ref[out, at + 256:at + 384] = vp[:, :128]
+
+
+def qkv_kernel(
+    rows_ref, place_ref, value_src_ref, wq_ref, wk_ref, wv_ref,
+    q_ref, k_ref, v_ref, kv_ref, normed_ref,
+):
+    for start in range(0, q_ref.shape[0], LOC):
+        key_value_block(
+            start, rows_ref, place_ref, value_src_ref, wk_ref, wv_ref, normed_ref,
+            k_ref, v_ref, kv_ref, 0,
+        )
         block = pl.ds(start, LOC)
-        q_ref[block, :] = fold_rows(normed, wq).astype(jnp.bfloat16)
-        key = fold_rows(normed, wk).astype(jnp.bfloat16)
-        value = jnp.where(spare, 1.0, fold_rows(normed, wv)).astype(jnp.bfloat16)
-        k_ref[block, :] = key
-        v_ref[block, :] = value
-        low = lax.broadcasted_iota(jnp.int32, (PHASE_ROWS, 128), 1) < 64
-        for phase in range(RATE):
-            kp = key[phase * PHASE_ROWS:(phase + 1) * PHASE_ROWS, phase * LANES:(phase + 1) * LANES]
-            vp = value[phase * PHASE_ROWS:(phase + 1) * PHASE_ROWS, phase * LANES:(phase + 1) * LANES]
-            out = pl.ds(start // RATE, PHASE_ROWS)
-            at = phase * PACKED
-            kv_ref[out, at:at + 128] = kp[:, :128]
-            kv_ref[out, at + 128:at + 256] = jnp.where(low, kp[:, 128:], vp[:, 128:])
-            kv_ref[out, at + 256:at + 384] = vp[:, :128]
-
-
-def near_kernel(where_ref, q_ref, k_ref, v_ref, near_ref):
-    live = where_ref[0] - pl.program_id(0) * LOC
+        q_ref[block, :] = fold_rows(normed_ref[block, :], wq_ref[...]).astype(jnp.bfloat16)
+
+
+def near_block(live, query, key, value):
     key_row = lax.broadcasted_iota(jnp.int32, (LOC, LOC), 1)
     query_row = lax.broadcasted_iota(jnp.int32, (LOC, LOC), 0)
     key_pos = (key_row & (PHASE_ROWS - 1)) * RATE + key_row // PHASE_ROWS
     allowed = (key_pos < live) | (key_row == query_row)
     bias = jnp.where(allowed, 0.0, MASKED)
-    query, key, value = q_ref[...], k_ref[...], v_ref[...]
     lane = lax.broadcasted_iota(jnp.int32, (1, LANES), 1)
     result = jnp.zeros((LOC, LANES), jnp.float32)
     for head in range(PER_PHASE):
@@ -112,19 +120,18 @@
         acc = fold_rows(weights.astype(jnp.bfloat16), value)
         result = jnp.where(value_lanes(head) | (lane == 128 + head), acc, result)
         result = jnp.where(lane == 132 + head, top, result)
-    near_ref[...] = result
-
-
-def far_kernel(where_ref, value_src_ref, q_ref, near_ref, kv_ref, out_ref, att_ref, sum_ref):
-    phase = pl.program_id(0)
-    row_count = q_ref.shape[0]
+    return result
+
+
+def near_kernel(where_ref, q_ref, k_ref, v_ref, near_ref):
+    live = where_ref[0] - pl.program_id(0) * LOC
+    near_ref[...] = near_block(live, q_ref[...], k_ref[...], v_ref[...])
+
+
+def far_phase(phase, where_ref, query, near_own, near, packed, value_src, att_ref, starts):
+    row_count = near.shape[0]
     sparse = row_count // RATE
-    key_count = kv_ref.shape[0] * kv_ref.shape[1]
-    lane = lax.broadcasted_iota(jnp.int32, (1, LANES), 1)
-    starts = [pl.multiple_of(base + phase * PHASE_ROWS, PHASE_ROWS) for base in range(0, row_count, LOC)]
-    query = jnp.concatenate([q_ref[pl.ds(at, PHASE_ROWS), :] for at in starts], axis=0)
-    near_own = jnp.concatenate([near_ref[pl.ds(at, PHASE_ROWS), :] for at in starts], axis=0)
-    packed = kv_ref[...].reshape(key_count, PACKED)
+    key_count = packed.shape[0]
     key = packed[:, :LANES]
     low = lax.broadcasted_iota(jnp.int32, (key_count, 128), 1) < 64
     middle = packed[:, 128:256]
@@ -135,7 +142,6 @@
     query_index = lax.broadcasted_iota(jnp.int32, (sparse, key_count), 0) + where_ref[2]
     allowed = (key_index * RATE + phase < where_ref[1]) | (key_index == query_index)
     bias = jnp.where(allowed, 0.0, MASKED)
-    near = near_ref[...]
     plain = jnp.zeros((row_count, LANES), jnp.float32)
     joined = jnp.zeros((sparse, LANES), jnp.float32)
     for head in range(PER_PHASE):
@@ -152,19 +158,48 @@
         best = jnp.maximum(top, near_top)
         near_coef = jnp.exp2((near_top - best) * EXP_SCALE)
         far_coef = jnp.exp2((top - best) * EXP_SCALE)
-        merged = (near_coef * near_own + far_coef * acc) / (near_coef * near_total + far_coef * total)
+        scale = 1.0 / (near_coef * near_total + far_coef * total)
+        merged = (near_coef * scale) * near_own + (far_coef * scale) * acc
         mine = value_lanes(head)
         joined = jnp.where(mine, merged, joined)
-        plain = jnp.where(mine, near / near[:, 128 + head:129 + head], plain)
+        plain = jnp.where(mine, near * (1.0 / near[:, 128 + head:129 + head]), plain)
     att_ref[...] = plain.astype(jnp.bfloat16)
     for block, at in enumerate(starts):
         att_ref[pl.ds(at, PHASE_ROWS), :] = joined[
             block * PHASE_ROWS:(block + 1) * PHASE_ROWS
         ].astype(jnp.bfloat16)
     place = lax.broadcasted_iota(jnp.int32, (D, LANES), 0)
-    spread = (place == value_src_ref[...]).astype(jnp.bfloat16)
-    added = lax.dot_general(
+    spread = (place == value_src).astype(jnp.bfloat16)
+    return lax.dot_general(
         att_ref[...], spread, (((1,), (1,)), ((), ())), preferred_element_type=jnp.float32
+    )
+
+
+def phase_starts(phase, row_count):
+    return [
+        pl.multiple_of(base + phase * PHASE_ROWS, PHASE_ROWS) for base in range(0, row_count, LOC)
+    ]
+
+
+def write_ordered(where_ref, sum_ref, out_ref):
+    position = lax.broadcasted_iota(jnp.int32, (LOC, LOC), 0)
+    row = lax.broadcasted_iota(jnp.int32, (LOC, LOC), 1)
+    order = (row == (position & (RATE - 1)) * PHASE_ROWS + position // RATE).astype(jnp.bfloat16)
+    for start in range(0, out_ref.shape[0], LOC):
+        block = pl.ds(start, LOC)
+        ordered = fold_rows(order, sum_ref[block, :].astype(jnp.bfloat16))
+        live = lax.broadcasted_iota(jnp.int32, (LOC, 1), 0) + start < where_ref[0]
+        out_ref[block, :] = jnp.where(live, ordered, 0.0).astype(jnp.bfloat16)
+
+
+def far_kernel(where_ref, value_src_ref, q_ref, near_ref, kv_ref, out_ref, att_ref, sum_ref):
+    phase = pl.program_id(0)
+    starts = phase_starts(phase, q_ref.shape[0])
+    query = jnp.concatenate([q_ref[pl.ds(at, PHASE_ROWS), :] for at in starts], axis=0)
+    near_own = jnp.concatenate([near_ref[pl.ds(at, PHASE_ROWS), :] for at in starts], axis=0)
+    packed = kv_ref[...].reshape(kv_ref.shape[0] * kv_ref.shape[1], PACKED)
+    added = far_phase(
+        phase, where_ref, query, near_own, near_ref[...], packed, value_src_ref[...], att_ref, starts
     )
 
     @pl.when(phase == 0)
@@ -177,14 +212,101 @@
 
     @pl.when(phase == RATE - 1)
     def _():
-        position = lax.broadcasted_iota(jnp.int32, (LOC, LOC), 0)
-        row = lax.broadcasted_iota(jnp.int32, (LOC, LOC), 1)
-        order = (row == (position & (RATE - 1)) * PHASE_ROWS + position // RATE).astype(jnp.bfloat16)
-        for start in range(0, row_count, LOC):
-            block = pl.ds(start, LOC)
-            ordered = fold_rows(order, sum_ref[block, :].astype(jnp.bfloat16))
-            live = lax.broadcasted_iota(jnp.int32, (LOC, 1), 0) + start < where_ref[0]
-            out_ref[block, :] = jnp.where(live, ordered, 0.0).astype(jnp.bfloat16)
+        write_ordered(where_ref, sum_ref, out_ref)
+
+
+def attend_kernel(
+    where_ref, rows_ref, place_ref, value_src_ref, wq_ref, wk_ref, wv_ref, out_ref,
+    normed_ref, q_ref, k_ref, v_ref, kv_ref, near_ref, att_ref, sum_ref, send_sem, recv_sem,
+):
+    seg, grp = lax.axis_index("seg"), lax.axis_index("grp")
+    seg_x = seg // 2 * 2 + 1 - seg % 2
+    seg_y = (seg + 2) % 4
+    seg_d = seg_y // 2 * 2 + 1 - seg_y % 2
+    row_count = out_ref.shape[0]
+    sparse = row_count // RATE
+    half = kv_ref.shape[1] // 2
+
+    barrier = pltpu.get_barrier_semaphore()
+    for target in (seg_x, seg_y):
+        pl.semaphore_signal(
+            barrier, inc=1, device_id=(target, grp), device_id_type=pl.DeviceIdType.MESH
+        )
+
+    def copy(index, owner, part, target):
+        rows = pl.ds(pl.multiple_of(owner * sparse, sparse), sparse)
+        block = kv_ref.at[rows, part * half:(part + 1) * half]
+        return pltpu.make_async_remote_copy(
+            src_ref=block,
+            dst_ref=block,
+            send_sem=send_sem.at[index],
+            recv_sem=recv_sem.at[index],
+            device_id=(target, grp),
+            device_id_type=pl.DeviceIdType.MESH,
+        )
+
+    plan = (
+        (seg, seg_x, 0, seg_x),
+        (seg, seg_y, 1, seg_y),
+        (seg, seg_x, 1, seg_x),
+        (seg, seg_y, 0, seg_y),
+        (seg_x, seg_d, 0, seg_y),
+        (seg_y, seg_d, 1, seg_x),
+    )
+
+    def outgoing(index):
+        sent, _, part, target = plan[index]
+        return copy(index, sent, part, target)
+
+    def arrived(index):
+        _, got, part, target = plan[index]
+        copy(index, got, part, target).wait_recv()
+
+    for start in range(0, row_count, LOC):
+        key_value_block(
+            start, rows_ref, place_ref, value_src_ref, wk_ref, wv_ref, normed_ref,
+            k_ref, v_ref, kv_ref, seg * sparse,
+        )
+    pl.semaphore_wait(barrier, 2)
+    for index in range(4):
+        outgoing(index).start()
+    q_ref[...] = fold_rows(normed_ref[...], wq_ref[...]).astype(jnp.bfloat16)
+
+    def near_rows(start):
+        block = pl.ds(start, LOC)
+
+        @pl.loop(0, RATE)
+        def _(phase):
+            lanes = pl.ds(pl.multiple_of(phase * LANES, LANES), LANES)
+            near_ref[block, lanes] = near_block(
+                where_ref[0] - start, q_ref[block, lanes], k_ref[block, lanes], v_ref[block, lanes]
+            )
+
+    near_rows(0)
+    for index in (0, 1):
+        arrived(index)
+        outgoing(index + 4).start()
+    for start in range(LOC, row_count, LOC):
+        near_rows(start)
+    for index in range(2, 6):
+        arrived(index)
+    sum_ref[...] = jnp.zeros_like(sum_ref)
+
+    @pl.loop(0, RATE)
+    def _(phase):
+        lanes = pl.ds(pl.multiple_of(phase * LANES, LANES), LANES)
+        starts = phase_starts(phase, row_count)
+        query = jnp.concatenate([q_ref[pl.ds(at, PHASE_ROWS), lanes] for at in starts], axis=0)
+        near_own = jnp.concatenate([near_ref[pl.ds(at, PHASE_ROWS), lanes] for at in starts], axis=0)
+        packed = kv_ref[:, pl.ds(pl.multiple_of(phase * PACKED, PACKED), PACKED)]
+        sum_ref[...] += far_phase(
+            phase, where_ref, query, near_own, near_ref[:, lanes], packed,
+            value_src_ref[:, lanes], att_ref, starts,
+        )
+
+    write_ordered(where_ref, sum_ref, out_ref)
+    for index in range(6):
+        outgoing(index).wait_send()
 
 
 def attention(rows, place, query_weight, key_weight, value_weight, valid_limit, row_count):
@@ -199,18 +321,54 @@
         seg_here * sparse,
     ]).astype(jnp.int32)
     key_src, value_src = (jnp.asarray(src) for src in lane_sources())
-    wide = jax.ShapeDtypeStruct((row_count, RATE * LANES), jnp.bfloat16)
     params = pltpu.CompilerParams(vmem_limit_bytes=VMEM_LIMIT)
     whole = pl.BlockSpec(memory_space=pltpu.VMEM)
     scalars = pl.BlockSpec(memory_space=pltpu.SMEM)
+    lane_weights = pl.pallas_call(
+        pick_weights_kernel,
+        out_shape=(jax.ShapeDtypeStruct((D, RATE * LANES), jnp.bfloat16),) * 3,
+        in_specs=[whole] * 5,
+        out_specs=(whole,) * 3,
+        compiler_params=params,
+        cost_estimate=pl.CostEstimate(
+            flops=6 * D * D * RATE * LANES, bytes_accessed=14 * D * D, transcendentals=0
+        ),
+        name="pick_weights",
+    )(key_src, value_src, query_weight, key_weight, value_weight)
+    lanes = (row_count, RATE * LANES)
+    wide = jax.ShapeDtypeStruct(lanes, jnp.bfloat16)
+    if (seg_count, lax.axis_size("grp")) == (4, 8):
+        return pl.pallas_call(
+            attend_kernel,
+            out_shape=jax.ShapeDtypeStruct((row_count, D), jnp.bfloat16),
+            in_specs=[scalars] + [whole] * 6,
+            out_specs=whole,
+            scratch_shapes=[
+                pltpu.VMEM((row_count, D), jnp.bfloat16),
+                pltpu.VMEM(lanes, jnp.bfloat16),
+                pltpu.VMEM(lanes, jnp.bfloat16),
+                pltpu.VMEM(lanes, jnp.bfloat16),
+                pltpu.VMEM((seg_count * sparse, RATE * PACKED), jnp.bfloat16),
+                pltpu.VMEM(lanes, jnp.float32),
+                pltpu.VMEM((row_count, LANES), jnp.bfloat16),
+                pltpu.VMEM((row_count, D), jnp.float32),
+                pltpu.SemaphoreType.DMA((6,)),
+                pltpu.SemaphoreType.DMA((6,)),
+            ],
+            compiler_params=pltpu.CompilerParams(
+                collective_id=1, has_side_effects=True, vmem_limit_bytes=VMEM_LIMIT
+            ),
+            name="attend",
+        )(where, rows, place, value_src, *lane_weights)
     query, key, value, packed = pl.pallas_call(
         qkv_kernel,
         out_shape=(wide, wide, wide, jax.ShapeDtypeStruct((sparse, RATE * PACKED), jnp.bfloat16)),
-        in_specs=[whole] * 7,
+        in_specs=[whole] * 6,
         out_specs=(whole,) * 4,
+        scratch_shapes=[pltpu.VMEM((row_count, D), jnp.bfloat16)],
         compiler_params=params,
         name="qkv",
-    )(rows, place, key_src, value_src, query_weight, key_weight, value_weight)
+    )(rows, place, value_src, *lane_weights)
     shared = lax.all_gather(packed, "seg", axis=0)
     tile = pl.BlockSpec((LOC, LANES), lambda block, phase: (block, phase))
     near = pl.pallas_call(

time: 296 us -> 262 us (0.89)
  waiting for transfers between devices: 95.2 us -> 62.3 us
  between operations: 14.1 us -> 0.75 us
  Pallas kernels: 165 us -> 175 us
    all_gather x1 -> x0, waiting for transfers between devices: 24.7 us -> none  [attention(): shared = lax.all_gather(packed, 'seg', axis=0)]
    pallas_call x3 -> x2, Pallas kernels: 53.2 us -> 63.3 us  [the longest x1 56.2 us: attention(): pl.pallas_call(attend_kernel, out_shape=jax.ShapeDtypeStruct((row_count,...]
    all_to_all x1, waiting for transfers between devices: 70.5 us -> 62.3 us  [shards(): lax.all_to_all(send_rows.reshape(devices, slot_cap, D), ('seg', 'grp'), s...]
  transfers between devices with their start and end apart: 3 -> 2, of which waited for: 2 -> 1; matrix products, arithmetic and copies ran while one was open for 1% -> 1% of each run, Pallas kernels for 43% -> 45%
where the time goes in v3:
time: 262 us
  Pallas kernels  175 us (67%)
  waiting for transfers between devices  62.3 us (24%)
  starting transfers between devices  14.3 us (5%)
  local copies, waits for them, and re-layouts  6.2 us (2%)
  other arithmetic  2.87 us (1%)
    pallas_call x1, Pallas kernels, gathered_send_rows(): pl.pallas_call(expert_kernel, out_shape=jax.ShapeDtypeStruct((slots, D),...  112 us
    all_to_all x1, waiting for transfers between devices, shards(): lax.all_to_all(send_rows.reshape(devices, slot_cap, D), ('seg', 'grp'), s...  62.3 us
    pallas_call x1, Pallas kernels, attention(): pl.pallas_call(attend_kernel, out_shape=jax.ShapeDtypeStruct((row_count,...  56.2 us
    all_to_all x1, starting transfers between devices, shards(): lax.all_to_all(send_place.reshape(devices, slot_cap), ('seg', 'grp'), spl...  7.3 us
    pallas_call x1, Pallas kernels, attention(): pl.pallas_call(pick_weights_kernel, out_shape=(jax.ShapeDtypeStruct((D, R...  7.11 us
    all_to_all x1, starting transfers between devices, shards(): lax.all_to_all(send_rows.reshape(devices, slot_cap, D), ('seg', 'grp'), s...  7.03 us
  transfers between devices with their start and end apart: 2, of which 1 were waited for; matrix products, arithmetic and copies ran while one was open for 1% of the time, Pallas kernels for 45%

profile of v3, /device:TPU:0, one launch (start us, length us, event | category | flops | bytes accessed | tf_op | source)
XLA Modules:
  0.0 262.2 jit_solution(16064006912228687224)
XLA Ops:
  0.0 0.7 fusion.10
  0.7 0.5 fusion.2
  1.3 0.0 copy-start.1
  1.3 0.9 select_reduce_fusion
  2.2 0.7 sub.38
  2.9 7.3 %all-to-all-start.1 = ((s32[32,1,64]{2,1,0:T(1,128)}), s32[32,1,64]{2,1,0:T(1,128)S(1)}, u32[]{:S(2)}, u32[]{:S(2)}) async-start(s32[32,1,64]{2,1,0:T(1,128)} %sub.38), calls=%async_computation.1 | async-start | bytes 32768 | tf_op jit(solution)/shard_map/all_to_all | solution.py:682
  10.2 0.0 copy-done.1
  10.2 111.9 %feed_forward.1 = bf16[2048,768]{1,0:T(8,128)(2,1)} custom-call(bf16[1024,1536]{1,0:T(8,128)(2,1)} %tokens_ref.1, bf16[48,2048]{1,0:T(8,128)(2,1)} %gate_ref.1, bf16[48,2048]{1,0:T(8,128)(2,1)} %up_ref.1, bf16[64,1536]{1,0:T(8,128)(2,1)} %down_ref.1, bf16[1536,768]{1,0:T(8,128)(2,1)} %proj_ref.1, s32[1,1024]{1,0:T(1,128)} %bitcast.12), custom_call_target="tpu_custom_call" | custom-call | tf_op jit(solution)/shard_map/feed_forward/pallas_call | solution.py:618
  122.1 0.0 all-to-all-done.1
  122.1 7.0 %all-to-all-start = ((bf16[32,64,768]{2,1,0:T(8,128)(2,1)}), bf16[32,64,768]{2,1,0:T(8,128)(2,1)S(1)}, u32[]{:S(2)}, u32[]{:S(2)}) async-start(bf16[32,64,768]{2,1,0:T(8,128)(2,1)} %bitcast.10), calls=%async_computation | async-start | bytes 6291456 | tf_op jit(solution)/shard_map/all_to_all | solution.py:696
  129.8 0.6 pad_add_fusion.where_ref
  130.4 7.1 %pick_weights.1 = (bf16[768,1024]{1,0:T(8,128)(2,1)}, bf16[768,1024]{1,0:T(8,128)(2,1)}, bf16[768,1024]{1,0:T(8,128)(2,1)}) custom-call(s32[1,1024]{1,0:T(1,128)} %constant.115.clone.key_src_ref, s32[1,1024]{1,0:T(1,128)} %constant.116.clone.value_src_ref, bf16[768,768]{1,0:T(8,128)(2,1)} %wq_ref.1, bf16[768,768]{1,0:T(8,128)(2,1)} %wk_ref.1, ...), custom_call_target="tpu_custom_call" | custom-call | flops 3623878656 | bytes 8257536 | tf_op jit(solution)/shard_map/pick_weights/pallas_call | solution.py:327
  137.5 0.5 broadcast.65
  138.1 0.6 reduce.3
  138.7 0.7 reshape.36.place_ref
  139.4 62.3 %all-to-all-done = bf16[32,64,768]{2,1,0:T(8,128)(2,1)S(1)} async-done(((bf16[32,64,768]{2,1,0:T(8,128)(2,1)}), bf16[32,64,768]{2,1,0:T(8,128)(2,1)S(1)}, u32[]{:S(2)}, u32[]{:S(2)}) %all-to-all-start) | async-done | bytes 3145760 | tf_op jit(solution)/shard_map/all_to_all | solution.py:696
  201.6 0.0 copy-start
  201.6 1.7 copy-done
  203.3 56.2 %attend.1 = bf16[1024,768]{1,0:T(8,128)(2,1)} custom-call(s32[3]{0:T(128)} %pad_add_fusion.where_ref, bf16[2048,768]{1,0:T(8,128)(2,1)} %bitcast.9, s32[1,2048]{1,0:T(1,128)} %reshape.36.place_ref, s32[1,1024]{1,0:T(1,128)} %constant.116.clone.value_src_ref, bf16[768,1024]{1,0:T(8,128)(2,1)} %get-tuple-element.8.wq_ref, ...), custom_call_target="tpu_custom_call" | custom-call | tf_op jit(solution)/shard_map/attend/pallas_call | solution.py:341
  259.5 2.7 %copy.15 = bf16[1,1024,768]{2,1,0:T(8,128)(2,1)} copy(bf16[1,1024,768]{2,1,0:T(8,128)(2,1)} %bitcast.11) | data formatting | bytes 3145728
  (2 shorter events, 0.0 us)
Async XLA Ops:
  1.3 8.9 %copy-start.1 = (s32[1024]{0:T(1024)}, s32[1024]{0:T(1024)S(1)}, u32[]{:S(2)}) copy-start(s32[1024]{0:T(1024)S(1)} %convert_add_fusion) | copy-start | bytes 12292
  2.9 119.2 %all-to-all-start.1 = ((s32[32,1,64]{2,1,0:T(1,128)}), s32[32,1,64]{2,1,0:T(1,128)S(1)}, u32[]{:S(2)}, u32[]{:S(2)}) async-start(s32[32,1,64]{2,1,0:T(1,128)} %sub.38), calls=%async_computation.1 | async-start | bytes 32768 | tf_op jit(solution)/shard_map/all_to_all | solution.py:682
  122.1 79.5 %all-to-all-start = ((bf16[32,64,768]{2,1,0:T(8,128)(2,1)}), bf16[32,64,768]{2,1,0:T(8,128)(2,1)S(1)}, u32[]{:S(2)}, u32[]{:S(2)}) async-start(bf16[32,64,768]{2,1,0:T(8,128)(2,1)} %bitcast.10), calls=%async_computation | async-start | bytes 6291456 | tf_op jit(solution)/shard_map/all_to_all | solution.py:696
  201.6 1.7 copy-start

commit v4 on v3

--- a/solution.py
+++ b/solution.py
@@ -407,11 +407,18 @@
     )(where, value_src, query, near, shared)
 
 
-def block_half(ref, rows, half):
-    if half is None:
-        return ref.at[rows, :]
-    width = ref.shape[1] // 2
-    return ref.at[rows, half * width:(half + 1) * width]
+def block_part(ref, rows, part):
+    width = ref.shape[1]
+    edge = width // 6 // 128 * 128
+    first, last = {
+        "all": (0, width),
+        "left": (0, width // 2),
+        "right": (width // 2, width),
+        "left_edge": (0, edge),
+        "middle": (edge, width - edge),
+        "right_edge": (width - edge, width),
+    }[part]
+    return ref.at[rows, first:last]
 
 
 def expert_kernel(
@@ -427,51 +434,58 @@
     gathered = (wide_ref, deep_ref)
     depth = (gate_ref.shape[0], down_ref.shape[0])
     copies = {
-        "up": (0, (seg, grp + 2), None),
-        "down": (9, (seg, grp - 2), None),
-        "x": (1, (seg_x, grp), None),
-        "y": (2, (seg_y, grp), None),
-        "xy": (3, (seg_y, grp), 0),
-        "yx": (4, (seg_x, grp), 1),
-        "own": (5, (seg, sibling), None),
-        "own_x": (6, (seg, sibling), None),
-        "own_y": (7, (seg, sibling), None),
-        "own_d": (8, (seg, sibling), None),
+        "up": (0, (seg, grp + 2), "all", "all"),
+        "down": (9, (seg, grp - 2), "all", "all"),
+        "x": (1, (seg_x, grp), "all", "all"),
+        "y": (2, (seg_y, grp), "all", "all"),
+        "xy": (3, (seg_y, grp), "left", "left_edge"),
+        "yx": (4, (seg_x, grp), "right", "right_edge"),
+        "own": (5, (seg, sibling), "all", "all"),
+        "own_x": (6, (seg, sibling), "all", "all"),
+        "own_y": (7, (seg, sibling), "all", "all"),
+        "own_d": (8, (seg, sibling), "all", "all"),
+        "mid_up": (10, (seg, grp + 2), "middle", "middle"),
+        "mid_down": (11, (seg, grp - 2), "middle", "middle"),
     }
     sent_block = {
         "up": seg, "down": seg, "x": seg, "y": seg, "xy": seg_x, "yx": seg_y,
         "own": seg, "own_x": seg_x, "own_y": seg_y, "own_d": seg_d,
+        "mid_up": seg_d, "mid_down": seg_d,
     }
     got_block = {
         "up": seg, "x": seg_x, "y": seg_y, "xy": seg_d, "yx": seg_d,
         "own": seg, "own_x": seg_x, "own_y": seg_y, "own_d": seg_d,
+        "mid_up": seg_d,
     }
+    landing = {"down": 0, "mid_up": 9, "mid_down": 9}
 
     def rows_of(which, block_seg, j, block_core):
         owner = block_seg * 8 + j * 2 + block_core
         return pl.ds(pl.multiple_of(owner * depth[which], 16), depth[which])
 
-    def outgoing(which, j, kind):
-        index, target, half = copies[kind]
-        block = block_half(gathered[which], rows_of(which, sent_block[kind], j, core), half)
+    def outgoing(which, j, kind, home=False):
+        index, target, *parts = copies[kind]
+        rows = rows_of(which, sent_block[kind], j, core)
+        block = block_part(gathered[which], rows, parts[0 if home else 1])
         return pltpu.make_async_remote_copy(
             src_ref=block,
             dst_ref=block,
             send_sem=send_sem.at[which, j, index],
-            recv_sem=recv_sem.at[which, j, 0 if kind == "down" else index],
+            recv_sem=recv_sem.at[which, j, landing.get(kind, index)],
             device_id=target,
             device_id_type=pl.DeviceIdType.MESH,
         )
 
-    def arrived(which, j, kind):
-        index, target, half = copies[kind]
+    def arrived(which, j, kind, home=False):
+        index, _, *parts = copies[kind]
         from_core = 1 - core if kind.startswith("own") else core
-        block = block_half(gathered[which], rows_of(which, got_block[kind], j, from_core), half)
+        rows = rows_of(which, got_block[kind], j, from_core)
+        block = block_part(gathered[which], rows, parts[0 if home else 1])
         pltpu.make_async_remote_copy(
             src_ref=block,
             dst_ref=block,
             send_sem=send_sem.at[which, j, index],
-            recv_sem=recv_sem.at[which, j, index],
+            recv_sem=recv_sem.at[which, j, landing.get(kind, index)],
             device_id=(seg, sibling),
             device_id_type=pl.DeviceIdType.MESH,
         ).wait_recv()
@@ -498,17 +512,23 @@
     def cross(which, k):
         def do(j, rising, falling):
             arrived(which, j, "x")
-            outgoing(which, j, "xy").start()
+            outgoing(which, j, "xy", k == 0).start()
             outgoing(which, j, "own_x").start()
             arrived(which, j, "y")
-            outgoing(which, j, "yx").start()
+            outgoing(which, j, "yx", k == 0).start()
             outgoing(which, j, "own_y").start()
         each_of_wave(k, do)
 
     def close(which, k):
         def do(j, rising, falling):
-            arrived(which, j, "xy")
-            arrived(which, j, "yx")
+            arrived(which, j, "xy", k == 0)
+            arrived(which, j, "yx", k == 0)
+            if k > 0:
+                arrived(which, j, "mid_up")
+            if rising:
+                pl.when(z < 3)(lambda: outgoing(which, j, "mid_up").start())
+            if falling:
+                pl.when(z > 0)(lambda: outgoing(which, j, "mid_down").start())
             outgoing(which, j, "own_d").start()
         each_of_wave(k, do)
 
@@ -601,10 +621,13 @@
     for which in range(2):
         for j in range(4):
             for kind in copies:
-                if kind == "up":
-                    pl.when((z < 3) & (z >= j))(lambda: outgoing(which, j, "up").wait_send())
-                elif kind == "down":
-                    pl.when((z > 0) & (z <= j))(lambda: outgoing(which, j, "down").wait_send())
+                if kind in ("up", "mid_up"):
+                    pl.when((z < 3) & (z >= j))(lambda: outgoing(which, j, kind).wait_send())
+                elif kind in ("down", "mid_down"):
+                    pl.when((z > 0) & (z <= j))(lambda: outgoing(which, j, kind).wait_send())
+                elif kind in ("xy", "yx"):
+                    pl.when(z == j)(lambda: outgoing(which, j, kind, True).wait_send())
+                    pl.when(z != j)(lambda: outgoing(which, j, kind).wait_send())
                 else:
                     outgoing(which, j, kind).wait_send()
 
@@ -626,8 +649,8 @@
             pltpu.VMEM((row_count, width), jnp.bfloat16),
             pltpu.VMEM((row_count, hidden_width), jnp.bfloat16),
             pltpu.VMEM((row_count, D), jnp.bfloat16),
+            pltpu.SemaphoreType.DMA((2, 4, 12)),
             pltpu.SemaphoreType.DMA((2, 4, 10)),
-            pltpu.SemaphoreType.DMA((2, 4, 9)),
         ],
         compiler_params=pltpu.CompilerParams(
             collective_id=0, has_side_effects=True, vmem_limit_bytes=VMEM_LIMIT
@@ -669,8 +692,6 @@
     target_grp = tile_rank // seg_tok
     target_seg = tile_rank % seg_tok // row_count
     target = target_seg * grp_count + target_grp
-    within = tile_rank % row_count
-    within = within // LOC * LOC + within % RATE * PHASE_ROWS + within % LOC // RATE
     onehot = target[:, None] == jnp.arange(devices, dtype=jnp.int32)[None, :]
     order = jnp.arange(row_count, dtype=jnp.int32)
     earlier = (order[None, :] < order[:, None]).astype(jnp.bfloat16)
@@ -678,14 +699,7 @@
     rank_within = jnp.sum(jnp.where(onehot, before, 0.0), axis=1).astype(jnp.int32)
     slot_index = target * slot_cap + rank_within
     filled = jnp.arange(slots, dtype=jnp.int32)[:, None] == slot_index[None, :]
-    send_place = jnp.sum(jnp.where(filled, within[None, :] + 1, 0), axis=1) - 1
-    got_place = lax.all_to_all(
-        send_place.reshape(devices, slot_cap),
-        ("seg", "grp"),
-        split_axis=0,
-        concat_axis=0,
-        tiled=True,
-    ).reshape(1, slots)
+    all_ranks = lax.all_gather(tile_rank, ("seg", "grp"), axis=0)
     if (seg_count, grp_count) == (4, 8):
         send_rows = gathered_send_rows(
             tile_tokens, gate_weight, up_weight, down_weight, proj_weight, slot_index, slots
@@ -693,6 +707,21 @@
     else:
         embedded = feed_forward(tile_tokens, gate_weight, up_weight, down_weight, proj_weight)
         send_rows = fold_rows(filled.astype(jnp.bfloat16), embedded).astype(jnp.bfloat16)
+    all_ranks, send_rows, query_weight, key_weight, value_weight = lax.optimization_barrier(
+        (all_ranks, send_rows, query_weight, key_weight, value_weight)
+    )
+    within = all_ranks - lax.axis_index("grp") * seg_tok - lax.axis_index("seg") * row_count
+    mine = (within >= 0) & (within < row_count)
+    mine_before = lax.dot_general(
+        mine.astype(jnp.bfloat16),
+        earlier,
+        (((1,), (1,)), ((), ())),
+        preferred_element_type=jnp.float32,
+    ).astype(jnp.int32)
+    row = within // LOC * LOC + within % RATE * PHASE_ROWS + within % LOC // RATE
+    got_slot = jnp.where(mine, mine_before, -1)[:, None, :]
+    here = got_slot == jnp.arange(slot_cap, dtype=jnp.int32)[None, :, None]
+    got_place = (jnp.sum(jnp.where(here, row[:, None, :] + 1, 0), axis=2) - 1).reshape(1, slots)
     got_rows = lax.all_to_all(
         send_rows.reshape(devices, slot_cap, D),
         ("seg", "grp"),

time: 262 us -> 294 us (1.12)
  blocking collectives: 0 us -> 44 us
  starting transfers between devices: 14.3 us -> 2.98 us
    all_gather x0 -> x1, blocking collectives: none -> 44 us  [shards(): all_ranks = lax.all_gather(tile_rank, ('seg', 'grp'), axis=0)]
    all_to_all x1 -> x0, starting transfers between devices: 7.3 us -> none  [shards(): lax.all_to_all(send_place.reshape(devices, slot_cap), ('seg', 'grp'), spl...]
    all_to_all x1, starting transfers between devices: 7.03 us -> 2.98 us  [shards(): lax.all_to_all(send_rows.reshape(devices, slot_cap, D), ('seg', 'grp'), s...]
  transfers between devices with their start and end apart: 2 -> 1, of which waited for: 1 -> 1; matrix products, arithmetic and copies ran while one was open for 1% -> 1% of each run, Pallas kernels for 45% -> 2%
where the time goes in v4:
time: 294 us
  Pallas kernels  175 us (60%)
  waiting for transfers between devices  61.4 us (21%)
  blocking collectives  44 us (15%)
  local copies, waits for them, and re-layouts  5.02 us (2%)
  other arithmetic  4.03 us (1%)
  starting transfers between devices  2.98 us (1%)
    pallas_call x1, Pallas kernels, gathered_send_rows(): pl.pallas_call(expert_kernel, out_shape=jax.ShapeDtypeStruct((slots, D),...  111 us
    all_to_all x1, waiting for transfers between devices, shards(): lax.all_to_all(send_rows.reshape(devices, slot_cap, D), ('seg', 'grp'), s...  61.4 us
    pallas_call x1, Pallas kernels, attention(): pl.pallas_call(attend_kernel, out_shape=jax.ShapeDtypeStruct((row_count,...  56.2 us
    all_gather x1, blocking collectives, shards(): all_ranks = lax.all_gather(tile_rank, ('seg', 'grp'), axis=0)  44 us
    pallas_call x1, Pallas kernels, attention(): pl.pallas_call(pick_weights_kernel, out_shape=(jax.ShapeDtypeStruct((D, R...  7.11 us
  transfers between devices with their start and end apart: 1, of which 1 were waited for; matrix products, arithmetic and copies ran while one was open for 1% of the time, Pallas kernels for 2%

profile of v4, /device:TPU:0, one launch (start us, length us, event | category | flops | bytes accessed | tf_op | source)
XLA Modules:
  0.0 293.9 jit_solution(1522739885463626388)
XLA Ops:
  0.0 0.7 fusion.26
  0.7 44.0 %all-gather = s32[32768]{0:T(1024)S(1)} all-gather(s32[1024]{0:T(1024)} %param.20), channel_id=2, replica_groups=mesh['seg'=4,'grp'=8] {'seg','grp'}, dimensions={0}, use_global_device_ids=true | all-gather | bytes 135168 | tf_op jit(solution)/shard_map/all_gather | solution.py:702
  44.7 0.5 fusion.5
  45.2 1.3 convert_add_fusion
  46.5 111.3 %feed_forward.1 = bf16[2048,768]{1,0:T(8,128)(2,1)} custom-call(bf16[1024,1536]{1,0:T(8,128)(2,1)} %tokens_ref.1, bf16[48,2048]{1,0:T(8,128)(2,1)} %gate_ref.1, bf16[48,2048]{1,0:T(8,128)(2,1)} %up_ref.1, bf16[64,1536]{1,0:T(8,128)(2,1)} %down_ref.1, bf16[1536,768]{1,0:T(8,128)(2,1)} %proj_ref.1, s32[1,1024]{1,0:T(1,128)} %bitcast.12), custom_call_target="tpu_custom_call" | custom-call | tf_op jit(solution)/shard_map/feed_forward/pallas_call | solution.py:641
  157.9 3.0 %all-to-all-start = ((bf16[32,64,768]{2,1,0:T(8,128)(2,1)}), bf16[32,64,768]{2,1,0:T(8,128)(2,1)S(1)}, u32[]{:S(2)}, u32[]{:S(2)}) async-start(bf16[32,64,768]{2,1,0:T(8,128)(2,1)} %bitcast.10), calls=%async_computation | async-start | bytes 6291456 | tf_op jit(solution)/shard_map/all_to_all | solution.py:725
  161.5 0.5 fusion.4
  162.1 0.3 fusion.9
  162.3 1.2 select_reduce_fusion
  163.5 0.7 sub.56.place_ref
  164.2 0.6 pad_add_fusion.where_ref
  164.8 7.1 %pick_weights.1 = (bf16[768,1024]{1,0:T(8,128)(2,1)}, bf16[768,1024]{1,0:T(8,128)(2,1)}, bf16[768,1024]{1,0:T(8,128)(2,1)}) custom-call(s32[1,1024]{1,0:T(1,128)} %constant.115.clone.key_src_ref, s32[1,1024]{1,0:T(1,128)} %constant.116.clone.value_src_ref, bf16[768,768]{1,0:T(8,128)(2,1)} %wq_ref, bf16[768,768]{1,0:T(8,128)(2,1)} %wk_ref, bf16[768,768]{1,0:T(8,128)(2,1)} %wv_ref), custom_call_target="tpu_custom_call" | custom-call | flops 3623878656 | bytes 8257536 | tf_op jit(solution)/shard_map/pick_weights/pallas_call | solution.py:327
  171.9 61.4 %all-to-all-done = bf16[32,64,768]{2,1,0:T(8,128)(2,1)S(1)} async-done(((bf16[32,64,768]{2,1,0:T(8,128)(2,1)}), bf16[32,64,768]{2,1,0:T(8,128)(2,1)S(1)}, u32[]{:S(2)}, u32[]{:S(2)}) %all-to-all-start) | async-done | bytes 3145760 | tf_op jit(solution)/shard_map/all_to_all | solution.py:725
  233.3 0.0 copy-start
  233.3 1.7 copy-done
  235.0 56.2 %attend.1 = bf16[1024,768]{1,0:T(8,128)(2,1)} custom-call(s32[3]{0:T(128)} %pad_add_fusion.where_ref, bf16[2048,768]{1,0:T(8,128)(2,1)} %bitcast.9, s32[1,2048]{1,0:T(1,128)} %sub.56.place_ref, s32[1,1024]{1,0:T(1,128)} %constant.116.clone.value_src_ref, bf16[768,1024]{1,0:T(8,128)(2,1)} %get-tuple-element.18.wq_ref, ...), custom_call_target="tpu_custom_call" | custom-call | tf_op jit(solution)/shard_map/attend/pallas_call | solution.py:341
  291.2 2.7 copy.15
  (2 shorter events, 0.0 us)
Async XLA Ops:
  157.9 75.4 %all-to-all-start = ((bf16[32,64,768]{2,1,0:T(8,128)(2,1)}), bf16[32,64,768]{2,1,0:T(8,128)(2,1)S(1)}, u32[]{:S(2)}, u32[]{:S(2)}) async-start(bf16[32,64,768]{2,1,0:T(8,128)(2,1)} %bitcast.10), calls=%async_computation | async-start | bytes 6291456 | tf_op jit(solution)/shard_map/all_to_all | solution.py:725
  233.3 1.7 copy-start
